TPU v7x, 256 devices: a whole 4x4x8 slice. The times are simulated.
256 devices in a mesh: gx: 8 (over z), gy: 16 (over y, x), gz: 2 (over core).
Axes of the slice: x: 4, y: 4, z: 8, core: 2. Of those that a mesh axis runs over, the one named last changes fastest.
Arguments:
- initial_state: float32 [4, 12, 256, 1024], P(None, 'gz', 'gy', 'gx'), may hold values from -6 to 6
- state_cotangent: float32 [4, 12, 256, 1024], P(None, 'gz', 'gy', 'gx'), may hold values from -6 to 6
- diffusion: float32 [12, 256, 1024], P('gz', 'gy', 'gx'), may hold values from 0.02 to 0.15
- weight_in: bfloat16 [40, 128], replicated, may hold values from -1 to 1
- weight_second: bfloat16 [128, 128], replicated, may hold values from -0.5 to 0.5
- weight_third: bfloat16 [128, 128], replicated, may hold values from -0.5 to 0.5
- weight_out: bfloat16 [128, 4], replicated, may hold values from -3 to 3
- biases_hidden: float32 [3, 128], replicated, may hold values from -3 to 3
- bias_out: float32 [4], replicated, may hold values from -4 to 4
Outputs:
- final_state: float32 [4, 12, 256, 1024], P(None, 'gz', 'gy', 'gx')
- initial_adjoint: float32 [4, 12, 256, 1024], P(None, 'gz', 'gy', 'gx')
- grad_weight_in: float32 [40, 128], replicated
- grad_weight_second: float32 [128, 128], replicated
- grad_weight_third: float32 [128, 128], replicated
- grad_weight_out: float32 [128, 4], replicated
- grad_biases: float32 [3, 128], replicated
- grad_bias_out: float32 [4], replicated
All inputs are finite; a program needn't handle non-finite values.
Results may differ from a plain program's by a relative error of at most 0.009.
Values sent between devices are 32-bit elements; how exact they have to be, the bound alone decides.
A program may use at most 64 MiB of HBM per device.

v0:
```python
import math

import jax
import jax.numpy as jnp
from jax import lax
from jax.sharding import PartitionSpec as P

time_step = 0.1
offsets = (
    (0, 0, 0),
    (0, 0, 1),
    (0, 0, -1),
    (0, 1, 0),
    (0, -1, 0),
    (1, 0, 0),
    (-1, 0, 0),
    (0, 1, 1),
    (1, 1, 0),
    (1, 0, 1),
)


def extended(block, sides, width):
    for axis, dim in sides:
        count = lax.axis_size(axis)
        forward = [(i, i + 1) for i in range(count - 1)]
        forward.append((count - 1, 0))
        backward = [(target, source) for source, target in forward]
        low = lax.ppermute(
            lax.slice_in_dim(block, block.shape[dim] - width, None, axis=dim), axis, forward
        )
        high = lax.ppermute(lax.slice_in_dim(block, 0, width, axis=dim), axis, backward)
        block = jnp.concatenate([low, block, high], axis=dim)
    return block


def contract(former, latter):
    return lax.dot_general(
        former, latter, (((0,), (0,)), ((), ())), preferred_element_type=jnp.float32
    )


def outer_sum(former, latter):
    return lax.dot_general(
        former, latter, (((1,), (1,)), ((), ())), preferred_element_type=jnp.float32
    )


def apply_back(weight, latter):
    return lax.dot_general(
        weight, latter, (((1,), (0,)), ((), ())), preferred_element_type=jnp.float32
    )


def silu_slope(values):
    sigmoid_value = jax.nn.sigmoid(values)
    return sigmoid_value * (1.0 + values * (1.0 - sigmoid_value))


def hidden_layers(features, weights, biases_hidden):
    pre_one = contract(weights[0], features) + biases_hidden[0][:, None]
    act_one = jax.nn.silu(pre_one).astype(jnp.bfloat16)
    pre_two = contract(weights[1], act_one) + biases_hidden[1][:, None]
    act_two = jax.nn.silu(pre_two).astype(jnp.bfloat16)
    pre_three = contract(weights[2], act_two) + biases_hidden[2][:, None]
    act_three = jax.nn.silu(pre_three).astype(jnp.bfloat16)
    return ((pre_one, pre_two, pre_three), (act_one, act_two, act_three))


def closure(features, weights, biases_hidden, bias_out):
    layered = hidden_layers(features, weights, biases_hidden)
    return contract(weights[3], layered[1][2]) + bias_out[:, None]


def backward(features, adjoint, weights, biases_hidden, own_mask):
    preacts, activations = hidden_layers(features, weights, biases_hidden)
    grad_out = (time_step * adjoint).astype(jnp.bfloat16)
    back_three = (apply_back(weights[3], grad_out) * silu_slope(preacts[2])).astype(jnp.bfloat16)
    back_two = (apply_back(weights[2], back_three) * silu_slope(preacts[1])).astype(jnp.bfloat16)
    back_one = (apply_back(weights[1], back_two) * silu_slope(preacts[0])).astype(jnp.bfloat16)
    feature_grad = apply_back(weights[0], back_one)
    bias_terms = jnp.stack(
        [
            jnp.sum(back_one.astype(jnp.float32), axis=1),
            jnp.sum(back_two.astype(jnp.float32), axis=1),
            jnp.sum(back_three.astype(jnp.float32), axis=1),
        ]
    )
    gradients = (
        outer_sum(features, back_one),
        outer_sum(activations[0], back_two),
        outer_sum(activations[1], back_three),
        outer_sum(activations[2], grad_out),
        bias_terms,
        jnp.sum(grad_out.astype(jnp.float32), axis=1),
    )
    return (feature_grad, gradients)


def window(padded, corner, extent):
    return lax.slice(
        padded,
        (0, corner[0], corner[1], corner[2]),
        (padded.shape[0], corner[0] + extent[0], corner[1] + extent[1], corner[2] + extent[2]),
    )


def inner_extent(padded):
    return (padded.shape[1] - 2, padded.shape[2] - 2, padded.shape[3] - 2)


def features_of(padded):
    extent = inner_extent(padded)
    stacked = jnp.stack(
        [
            window(padded, (1 + offset[0], 1 + offset[1], 1 + offset[2]), extent)
            for offset in offsets
        ]
    )
    channels = len(offsets) * padded.shape[0]
    flat = stacked.reshape(channels, extent[0], extent[1] * extent[2]).astype(jnp.bfloat16)
    return jnp.moveaxis(flat, 1, 0)


def laplace_of(padded):
    extent = inner_extent(padded)
    summed = -6.0 * window(padded, (1, 1, 1), extent)
    for offset in offsets[1:7]:
        summed = summed + window(padded, (1 + offset[0], 1 + offset[1], 1 + offset[2]), extent)
    return summed


def advance(padded, diffusion, weights, biases_hidden, bias_out):
    extent = inner_extent(padded)
    fields = padded.shape[0]
    features = features_of(padded)
    closed = lax.map(
        lambda plane_cells: closure(plane_cells, weights, biases_hidden, bias_out), features
    )
    closed = jnp.moveaxis(closed, 0, 1).reshape((fields, extent[0], extent[1], extent[2]))
    state = window(padded, (1, 1, 1), extent)
    return state + diffusion * laplace_of(padded) + time_step * closed


def sweep(features, adjoints, weights, biases_hidden):
    fields = weights[3].shape[1]
    hidden = weights[3].shape[0]
    inputs_count = weights[0].shape[0]

    def one_plane(running, inputs):
        own_mask = None
        feature_grad, gradients = backward(inputs[0], inputs[1], weights, biases_hidden, own_mask)
        return (jax.tree.map(jnp.add, running, gradients), feature_grad)

    start_grads = (
        jnp.zeros((inputs_count, hidden), jnp.float32),
        jnp.zeros((hidden, hidden), jnp.float32),
        jnp.zeros((hidden, hidden), jnp.float32),
        jnp.zeros((hidden, fields), jnp.float32),
        jnp.zeros((3, hidden), jnp.float32),
        jnp.zeros((fields,), jnp.float32),
    )
    scanned = (features, adjoints)
    return lax.scan(one_plane, start_grads, scanned)


def fold_back(buffer):
    widened = extended(buffer, (("gx", 3),), 1)
    count_inner = buffer.shape[3] - 2
    interior = widened[:, :, :, 2 : count_inner + 2]
    interior = (
        interior.at[:, :, :, 0]
        .add(widened[:, :, :, 0])
        .at[:, :, :, count_inner - 1]
        .add(widened[:, :, :, count_inner + 3])
    )
    widened = extended(interior, (("gy", 2),), 1)
    count_inner = interior.shape[2] - 2
    interior = widened[:, :, 2 : count_inner + 2, :]
    interior = (
        interior.at[:, :, 0, :]
        .add(widened[:, :, 0, :])
        .at[:, :, count_inner - 1, :]
        .add(widened[:, :, count_inner + 3, :])
    )
    widened = extended(interior, (("gz", 1),), 1)
    count_inner = interior.shape[1] - 2
    interior = widened[:, 2 : count_inner + 2, :, :]
    interior = (
        interior.at[:, 0, :, :]
        .add(widened[:, 0, :, :])
        .at[:, count_inner - 1, :, :]
        .add(widened[:, count_inner + 3, :, :])
    )
    return interior


def retreat(stored, adjoint, diffusion, weights, biases_hidden):
    fields = adjoint.shape[0]
    extent = (adjoint.shape[1], adjoint.shape[2], adjoint.shape[3])
    inputs_count = weights[0].shape[0]
    features = features_of(stored)
    adjoint_planes = jnp.moveaxis(adjoint.reshape(fields, extent[0], extent[1] * extent[2]), 1, 0)
    gradients, feature_grads = sweep(features, adjoint_planes, weights, biases_hidden)
    feature_grads = jnp.moveaxis(feature_grads, 0, 1).reshape(
        (inputs_count, extent[0], extent[1], extent[2])
    )
    spread = diffusion[None] * adjoint
    buffer = jnp.zeros((fields, extent[0] + 2, extent[1] + 2, extent[2] + 2), jnp.float32)
    buffer = buffer.at[:, 1 : 1 + extent[0], 1 : 1 + extent[1], 1 : 1 + extent[2]].add(
        -6.0 * spread
    )
    for offset in offsets[1:7]:
        buffer = buffer.at[
            :,
            1 + offset[0] : 1 + offset[0] + extent[0],
            1 + offset[1] : 1 + offset[1] + extent[1],
            1 + offset[2] : 1 + offset[2] + extent[2],
        ].add(spread)
    for number in range(len(offsets)):
        offset = offsets[number]
        buffer = buffer.at[
            :,
            1 + offset[0] : 1 + offset[0] + extent[0],
            1 + offset[1] : 1 + offset[1] + extent[1],
            1 + offset[2] : 1 + offset[2] + extent[2],
        ].add(feature_grads[fields * number : fields * (number + 1)])
    return (adjoint + fold_back(buffer), gradients)


def on_device(
    initial_state,
    state_cotangent,
    diffusion,
    weight_in,
    weight_second,
    weight_third,
    weight_out,
    biases_hidden,
    bias_out,
):
    weights = (weight_in, weight_second, weight_third, weight_out)
    depth = 1

    def extend(grid_field):
        return extended(grid_field, (("gx", 3), ("gy", 2), ("gz", 1)), depth)

    first_padded = extend(initial_state)
    middle = advance(first_padded, diffusion, weights, biases_hidden, bias_out)
    second_padded = extend(middle)
    final_state = advance(second_padded, diffusion, weights, biases_hidden, bias_out)
    adjoint_middle, later_grads = retreat(
        second_padded, state_cotangent, diffusion, weights, biases_hidden
    )
    initial_adjoint, earlier_grads = retreat(
        first_padded, adjoint_middle, diffusion, weights, biases_hidden
    )
    local_grads = jax.tree.map(jnp.add, later_grads, earlier_grads)
    totals = lax.psum(
        (
            local_grads[0],
            local_grads[1],
            local_grads[2],
            local_grads[3],
            local_grads[4],
            local_grads[5],
        ),
        ("gx", "gy", "gz"),
    )
    cells = (
        initial_state.shape[1]
        * initial_state.shape[2]
        * initial_state.shape[3]
        * lax.axis_size("gx")
        * lax.axis_size("gy")
        * lax.axis_size("gz")
    )
    grad_scale = 1.0 / (time_step * math.sqrt(float(cells)))
    return (
        final_state,
        initial_adjoint,
        totals[0] * grad_scale,
        totals[1] * grad_scale,
        totals[2] * grad_scale,
        totals[3] * grad_scale,
        totals[4] * grad_scale,
        totals[5] * grad_scale,
    )


def solution(mesh):
    placed = (
        P(None, "gz", "gy", "gx"),
        P(None, "gz", "gy", "gx"),
        P("gz", "gy", "gx"),
        P(),
        P(),
        P(),
        P(),
        P(),
        P(),
    )
    return jax.shard_map(
        on_device,
        mesh=mesh,
        in_specs=placed,
        out_specs=(
            P(None, "gz", "gy", "gx"),
            P(None, "gz", "gy", "gx"),
            P(),
            P(),
            P(),
            P(),
            P(),
            P(),
        ),
        check_vma=False,
    )
```

profile of v0, /device:TPU:1, one launch (start us, length us, event | category | flops | bytes accessed | tf_op | source)
XLA Modules:
  0.0 880.8 jit_solution(7101352214182080844)
XLA Ops:
  17.9 7.8 scatter-add.155
  27.2 7.8 scatter-add.159
  35.1 7.8 scatter-add.160
  43.8 7.8 scatter-add.161
  69.8 13.5 %while.112 = (s32[]{:T(128)}, f32[6,4,2048]{2,1,0:T(4,128)S(1)}, bf16[6,40,2048]{2,1,0:T(8,128)(2,1)}, bf16[40,128]{1,0:T(8,128)(2,1)S(1)}, f32[3,128]{1,0:T(4,1...) while((s32[]{:T(128)}, f32[6,4,2048]{2,1,0:T(4,128)S(1)}, ...), condition=%wide.region_1.2_spmd, body=%wide.region_0.1_spmd.sunk | while | flops 162013184 | bytes 1327221 | solution.py:137
  116.4 47.8 %while.114 = (s32[]{:T(128)}, f32[40,128]{1,0:T(8,128)S(1)}, f32[128,128]{1,0:T(8,128)S(1)}, f32[128,128]{1,0:T(8,128)S(1)}, f32[128,4]{0,1:T(4,128)}, /*index=5...) while((s32[]{:T(128)}, f32[40,128]{1,0:T(8,128)S(1)}, ...), condition=%wide.region_9.10_spmd.clone, body=%wide.region_4.9_spmd.clone.sunk | while | flops 483242112 | bytes 16564084 | solution.py:164
  186.7 8.5 scatter-add.165
  196.9 8.5 scatter-add.166
  211.2 8.5 scatter-add.170
  221.4 8.5 scatter-add.171
  231.7 8.5 scatter-add.174
  241.9 8.5 scatter-add.175
  252.1 8.5 scatter-add.176
  262.4 8.7 scatter-add.179
  272.8 8.5 scatter-add.180
  283.1 30.6 %while.113 = (s32[]{:T(128)}, f32[6,4,2048]{2,1,0:T(4,128)}, bf16[6,40,2048]{2,1,0:T(8,128)(2,1)S(1)}, bf16[40,128]{1,0:T(8,128)(2,1)S(1)}, f32[3,128]{1,0:T(4,1...) while((s32[]{:T(128)}, f32[6,4,2048]{2,1,0:T(4,128)}, ...), condition=%wide.region_3.4_spmd, body=%wide.region_2.3_spmd.sunk | while | flops 162013184 | bytes 1327221 | solution.py:137
  344.9 8.2 scatter-add.194
  354.5 7.8 scatter-add.196
  362.5 7.8 scatter-add.199
  370.5 7.8 scatter-add.200
  378.4 7.8 scatter-add.201
  386.5 52.1 %while.115 = (s32[]{:T(128)}, f32[40,128]{1,0:T(8,128)S(1)}, f32[128,128]{1,0:T(8,128)S(1)}, f32[128,128]{1,0:T(8,128)S(1)}, f32[128,4]{0,1:T(4,128)}, /*index=5...) while((s32[]{:T(128)}, f32[40,128]{1,0:T(8,128)S(1)}, ...), condition=%wide.region_15.16_spmd.clone, body=%wide.region_10.15_spmd.clone.sunk | while | flops 483242112 | bytes 16564084 | solution.py:164
  439.9 80.0 %all-reduce.2 = (f32[40,128]{1,0:T(8,128)S(1)}, f32[128,4]{0,1:T(4,128)S(1)}, f32[3,128]{1,0:T(4,128)S(1)}, f32[4]{0:T(128)S(1)}) all-reduce(f32[40,128]{1,0:T(8,128)S(1)} %add.755, f32[128,4]{0,1:T(4,128)S(1)} %add.758, f32[3,128]{1,0:T(4,128)S(1)} %add.759, f32[4]{0:T(128)S(1)} %add.760), channel_id=1, replica_groups=mesh['gx'=8,'gy'=16,'gz'=2] {'gx','gy','gz'}, use_global_device_ids=true, to_apply=%region_16.17 | all-reduce | flops 6020 | bytes 48160 | tf_op jit(solution)/shard_map/psum | solution.py:259
  527.9 7.8 scatter-add.204
  535.9 7.8 scatter-add.205
  545.1 7.8 scatter-add.209
  553.1 7.8 scatter-add.210
  561.1 7.8 scatter-add.211
  569.0 7.8 scatter-add.214
  577.0 7.8 scatter-add.215
  585.0 7.8 scatter-add.216
  634.3 237.9 %all-reduce.6.cloned.1.call-done = (f32[128,128]{1,0:T(8,128)}, f32[128,128]{1,0:T(8,128)}) async-done(((f32[128,128]{1,0:T(8,128)}, f32[128,128]{1,0:T(8,128)}), (f32[128,128]{1,0:T(8,128)}, f32[128,128]{1,0:T(8,128)})) %all-reduce.6.cloned.1.call-update) | async-done | bytes 131088 | tf_op jit(solution)/shard_map/psum | solution.py:259
  (588 shorter events, 335.6 us)
Async XLA Ops:
  7.2 18.6 %copy-start.1 = (f32[6,16,128]{2,1,0:T(8,128)S(1)}, f32[6,16,128]{2,1,0:T(8,128)}, u32[]{:S(2)}) copy-start(f32[6,16,128]{2,1,0:T(8,128)} %param.111) | copy-start | bytes 147460
  7.2 18.6 %copy-start.2 = (f32[4,6,16,128]{3,2,1,0:T(8,128)S(1)}, f32[4,6,16,128]{3,2,1,0:T(8,128)}, u32[]{:S(2)}) copy-start(f32[4,6,16,128]{3,2,1,0:T(8,128)} %param.110) | copy-start | bytes 589828
  7.2 865.0 %all-reduce.6.cloned.1.call-start = ((), (), s32[]{:S(2)}) async-start(), calls=%async_computation | async-start | bytes 262144 | tf_op jit(solution)/shard_map/psum | solution.py:259
  8.4 43.2 %collective-permute-start.1 = (f32[4,6,16,1]{3,2,0,1:T(8,128)S(1)}, f32[4,6,16,1]{3,2,0,1:T(8,128)S(1)}, u32[]{:S(2)}, u32[]{:S(2)}) collective-permute-start(f32[4,6,16,1]{3,2,0,1:T(8,128)S(1)} %get-tuple-element.1130), channel_id=1, source_target_pairs={{0,32},{32,64},{64,96},{96,128},{128,160},{160,192},{192,224},{224... | collective-permute-start | bytes 4616 | tf_op jit(solution)/shard_map/ppermute | solution.py:29
  11.0 40.7 %collective-permute-start = (f32[4,6,16,1]{3,2,0,1:T(8,128)S(1)}, f32[4,6,16,1]{3,2,0,1:T(8,128)S(1)}, u32[]{:S(2)}, u32[]{:S(2)}) collective-permute-start(f32[4,6,16,1]{3,2,0,1:T(8,128)S(1)} %get-tuple-element.1131), channel_id=1, source_target_pairs={{32,0},{64,32},{96,64},{128,96},{160,128},{192,160},{224,192},{0,2... | collective-permute-start | bytes 4616 | tf_op jit(solution)/shard_map/ppermute | solution.py:32
  51.9 6.6 collective-permute-start.3
  53.2 5.3 collective-permute-start.2
  58.6 5.1 collective-permute-start.5
  60.3 2.3 collective-permute-start.4
  85.8 11.6 %collective-permute-start.7 = (f32[4,6,16,1]{3,2,0,1:T(8,128)S(1)}, f32[4,6,16,1]{3,2,0,1:T(8,128)S(1)}, u32[]{:S(2)}, u32[]{:S(2)}) collective-permute-start(f32[4,6,16,1]{3,2,0,1:T(8,128)S(1)} %get-tuple-element.1128), channel_id=1, source_target_pairs={{0,32},{32,64},{64,96},{96,128},{128,160},{160,192},{192,224},{224... | collective-permute-start | bytes 4616 | tf_op jit(solution)/shard_map/ppermute | solution.py:29
  85.9 11.5 %collective-permute-start.6 = (f32[4,6,16,1]{3,2,0,1:T(8,128)S(1)}, f32[4,6,16,1]{3,2,0,1:T(8,128)S(1)}, u32[]{:S(2)}, u32[]{:S(2)}) collective-permute-start(f32[4,6,16,1]{3,2,0,1:T(8,128)S(1)} %get-tuple-element.1129), channel_id=1, source_target_pairs={{32,0},{64,32},{96,64},{128,96},{160,128},{192,160},{224,192},{0,2... | collective-permute-start | bytes 4616 | tf_op jit(solution)/shard_map/ppermute | solution.py:32
  97.6 6.7 collective-permute-start.9
  97.7 6.6 collective-permute-start.8
  104.5 4.5 collective-permute-start.11
  106.0 1.8 collective-permute-start.10
  282.4 34.2 %collective-permute-start.12 = (f32[4,8,18,1]{3,2,0,1:T(8,128)}, f32[4,8,18,1]{3,2,0,1:T(8,128)}, u32[]{:S(2)}, u32[]{:S(2)}) collective-permute-start(f32[4,8,18,1]{3,2,0,1:T(8,128)} %get-tuple-element.1109), channel_id=1, source_target_pairs={{0,32},{32,64},{64,96},{96,128},{128,160},{160,192},{192,224},{224... | collective-permute-start | bytes 6920 | tf_op jit(solution)/shard_map/ppermute | solution.py:29
  313.8 10.8 %collective-permute-start.13 = (f32[4,8,18,1]{3,2,0,1:T(8,128)}, f32[4,8,18,1]{3,2,0,1:T(8,128)}, u32[]{:S(2)}, u32[]{:S(2)}) collective-permute-start(f32[4,8,18,1]{3,2,0,1:T(8,128)} %get-tuple-element.1108), channel_id=1, source_target_pairs={{32,0},{64,32},{96,64},{128,96},{160,128},{192,160},{224,192},{0,2... | collective-permute-start | bytes 6920 | tf_op jit(solution)/shard_map/ppermute | solution.py:32
  320.8 19.4 %copy-start.16 = (f32[4,6,1,130]{3,2,0,1:T(1,128)S(1)}, f32[4,6,1,130]{3,2,0,1:T(1,128)}, u32[]{:S(2)}) copy-start(f32[4,6,1,130]{3,2,0,1:T(1,128)} %copy-done.15) | copy-start | bytes 37444
  320.8 19.4 %copy-start.18 = (f32[4,6,1,130]{3,2,0,1:T(1,128)S(1)}, f32[4,6,1,130]{3,2,0,1:T(1,128)}, u32[]{:S(2)}) copy-start(f32[4,6,1,130]{3,2,0,1:T(1,128)} %copy-done.17) | copy-start | bytes 37444
  320.8 19.3 %copy-start.21 = (f32[4,1,18,130]{3,2,0,1:T(8,128)S(1)}, f32[4,1,18,130]{3,2,0,1:T(8,128)}, u32[]{:S(2)}) copy-start(f32[4,1,18,130]{3,2,0,1:T(8,128)} %copy-done.20) | copy-start | bytes 112324
  331.0 6.4 collective-permute-start.14
  331.4 6.2 collective-permute-start.15
  337.7 4.9 collective-permute-start.16
  342.5 1.3 collective-permute-start.17
  386.5 52.1 %copy-start.24 = (f32[4]{0:T(128)S(1)}, f32[4]{0:T(128)}, u32[]{:S(2)}) copy-start(f32[4]{0:T(128)} %get-tuple-element.834) | copy-start | bytes 52
  386.5 52.7 %copy-start.29 = (f32[128,4]{0,1:T(4,128)S(1)}, f32[128,4]{0,1:T(4,128)}, u32[]{:S(2)}) copy-start(f32[128,4]{0,1:T(4,128)} %get-tuple-element.830) | copy-start | bytes 6148
  601.0 11.0 %collective-permute-start.18 = (f32[4,8,18,1]{3,2,0,1:T(8,128)S(1)}, f32[4,8,18,1]{3,2,0,1:T(8,128)S(1)}, u32[]{:S(2)}, u32[]{:S(2)}) collective-permute-start(f32[4,8,18,1]{3,2,0,1:T(8,128)S(1)} %get-tuple-element.1107), channel_id=1, source_target_pairs={{0,32},{32,64},{64,96},{96,128},{128,160},{160,192},{192,224},{224... | collective-permute-start | bytes 6920 | tf_op jit(solution)/shard_map/ppermute | solution.py:29
  602.0 13.2 %collective-permute-start.19 = (f32[4,8,18,1]{3,2,0,1:T(8,128)S(1)}, f32[4,8,18,1]{3,2,0,1:T(8,128)S(1)}, u32[]{:S(2)}, u32[]{:S(2)}) collective-permute-start(f32[4,8,18,1]{3,2,0,1:T(8,128)S(1)} %get-tuple-element.1106), channel_id=1, source_target_pairs={{32,0},{64,32},{96,64},{128,96},{160,128},{192,160},{224,192},{0,2... | collective-permute-start | bytes 6920 | tf_op jit(solution)/shard_map/ppermute | solution.py:32
  620.7 6.0 collective-permute-start.20
  621.4 5.7 collective-permute-start.21
  627.2 5.2 collective-permute-start.22
  632.3 1.3 collective-permute-start.23
  (70 other events, 157.9 us)
Sparse Core Ops, SparseCore 0:
  632.4 239.7 all-reduce.5
where the time goes:
time: 892 us; the launch traced here: 881 us
  local copies, waits for them, and re-layouts  308 us (35%)
  waiting for transfers between devices  253 us (28%)
  matrix products  111 us (12%)
  blocking collectives  80 us (9%)
  other arithmetic  66.8 us (7%)
  starting transfers between devices  45.5 us (5%)
  between operations  15.6 us (2%)
    psum x1, waiting for transfers between devices, on_device(): lax.psum((local_grads[0], local_grads[1], local_grads[2], local_grads[3],...  238 us
    scatter-add x32, local copies, waits for them, and re-layouts, retreat(): buffer = buffer.at[:, 1 + offset[0]:1 + offset[0] + extent[0], 1 + offset...  232 us
    psum x1, blocking collectives, on_device(): lax.psum((local_grads[0], local_grads[1], local_grads[2], local_grads[3],...  80 us
    dot_general x60, matrix products, contract(): lax.dot_general(former, latter, (((0,), (0,)), ((), ())), preferred_eleme...  60.7 us
    ppermute x12, starting transfers between devices, extended(): lax.ppermute(lax.slice_in_dim(block, 0, width, axis=dim), axis, backward)  32.1 us
    dot_general x48, matrix products, apply_back(): lax.dot_general(weight, latter, (((1,), (0,)), ((), ())), preferred_eleme...  28.5 us
    another operation x24, local copies, waits for them, and re-layouts  25.2 us
    dot_general x48, matrix products, outer_sum(): lax.dot_general(former, latter, (((1,), (1,)), ((), ())), preferred_eleme...  21.5 us
  transfers between devices with their start and end apart: 25, of which 8 were waited for; matrix products, arithmetic and copies ran while one was open for 11% of the time, Pallas kernels for 0%

commit v1 on v0

v1 whole, which is shorter than its diff:
```python
import functools
import math

import jax
import jax.numpy as jnp
from jax import lax
from jax.experimental import pallas as pl
from jax.experimental.pallas import tpu as pltpu
from jax.sharding import PartitionSpec as P

bf16 = jnp.bfloat16
f32 = jnp.float32
MESH = pl.DeviceIdType.MESH

time_step = 0.1
FIELDS = 4
STENCIL = 10
PLANES = 6
ROWS = 64
LANES = 128
WIDE = 1024
HID = 128
SUMS = 384
SUBS = 2


def mm(former, latter):
    return lax.dot_general(former, latter, (((1,), (0,)), ((), ())), preferred_element_type=f32)


def mm_cells(former, latter):
    return lax.dot_general(former, latter, (((1,), (1,)), ((), ())), preferred_element_type=f32)


def lane_index(rows):
    return lax.broadcasted_iota(jnp.int32, (rows, LANES), 1)


def pack_lane(plane, lane, base, onto):
    index = lane_index(8)
    for part in range(8):
        moved = pltpu.roll(plane[8 * part : 8 * part + 8], (base + part - lane) % LANES, 1)
        onto = jnp.where(index == base + part, moved, onto)
    return onto


def unpack_lane(packed, base, lane):
    return jnp.concatenate(
        [pltpu.roll(packed, (lane - base - part) % LANES, 1) for part in range(8)], axis=0
    )


def rows_up(plane, first):
    return jnp.concatenate([first, plane[: ROWS - 4]], axis=0)


def rows_down(plane, last):
    return jnp.concatenate([plane[4:], last], axis=0)


def wide_of(plane):
    return jnp.concatenate([plane[8 * part : 8 * part + 8] for part in range(8)], axis=1)


def plane_of(wide):
    return jnp.concatenate(
        [wide[:, LANES * part : LANES * (part + 1)] for part in range(8)], axis=0
    )


def side_by_side(stacked):
    return jnp.concatenate([stacked[:HID], stacked[HID:]], axis=1)


def stacked_of(beside):
    half = beside.shape[1] // 2
    return jnp.concatenate([beside[:, :half], beside[:, half:]], axis=0)


def silu_parts(half):
    turned = jnp.tanh(half)
    raised = 1.0 + turned
    value = half * raised
    slope = raised * (1.0 - half * turned) + value
    return value.astype(bf16), slope.astype(bf16)


def kernel(
    sizes,
    scale,
    state_in,
    cot_in,
    diff_in,
    w_in,
    w_second,
    w_third,
    w_out,
    biases,
    bias_out,
    final_out,
    adjoint_out,
    g_in_out,
    g_second_out,
    g_third_out,
    g_readout_out,
    g_biases_out,
    g_bias_out_out,
    st,
    p_first,
    p_last,
    x_lo,
    x_hi,
    xy_hi,
    y_lo,
    y_hi,
    spread4,
    cot,
    adj_mid,
    staged,
    feats,
    acts,
    slopes,
    q,
    pa_last,
    pa_first,
    y_tiles,
    z_up,
    xa,
    xb,
    xya,
    ya,
    yb,
    l_one,
    l_two,
    l_three,
    l_out,
    v_out,
    v_three,
    v_two,
    v_one,
    square,
    g_one,
    g_two,
    g_three,
    g_four,
    sums,
    landed_a,
    landed_b,
    total,
    f_send,
    f_recv,
    f_send_z,
    f_recv_z,
    b_send,
    b_recv,
    b_send_z,
    b_recv_z,
    a_send,
    a_recv,
):
    nx, ny, nz = sizes
    gx, gy, gz = lax.axis_index("gx"), lax.axis_index("gy"), lax.axis_index("gz")
    right, left = lax.rem(gx + 1, nx), lax.rem(gx + nx - 1, nx)
    above, below = lax.rem(gy + 1, ny), lax.rem(gy + ny - 1, ny)
    other = 1 - gz
    group = nx * nz
    mine = gx * nz + gz
    share = SUMS // group

    def member(place):
        return (lax.div(place, nz), gy, lax.rem(place, nz))

    barrier = pltpu.get_barrier_semaphore()

    def greet(device):
        pl.semaphore_signal(barrier, inc=1, device_id=device, device_id_type=MESH)

    for device in ((right, above, gz), (left, below, gz), (gx, above, other), (gx, below, other)):
        greet(device)

    def greet_group(step, carry):
        greet(member(lax.rem(mine + step, group)))
        return carry

    lax.fori_loop(1, group, greet_group, 0)

    def greet_column(step, carry):
        greet((gx, lax.rem(gy + step, ny), gz))
        return carry

    lax.fori_loop(1, ny, greet_column, 0)

    def copy(source, target, send, recv, device):
        return pltpu.make_async_remote_copy(
            src_ref=source,
            dst_ref=target,
            send_sem=send,
            recv_sem=recv,
            device_id=device,
            device_id_type=MESH,
        )

    def field_copies(e, z):
        send, recv = f_send, f_recv
        return (
            copy(p_last.at[e, z], x_lo.at[e, z], send.at[e, 0, z], recv.at[e, 0, z], (right, gy, gz)),
            copy(p_first.at[e, z], x_hi.at[e, z], send.at[e, 1, z], recv.at[e, 1, z], (left, gy, gz)),
            copy(p_first.at[e, z], xy_hi.at[e, z], send.at[e, 2, z], recv.at[e, 2, z], (left, below, gz)),
            copy(st.at[e, z + 1, pl.ds(56, 8)], y_lo.at[e, z], send.at[e, 3, z], recv.at[e, 3, z], (gx, above, gz)),
            copy(st.at[e, z + 1, pl.ds(0, 8)], y_hi.at[e, z], send.at[e, 4, z], recv.at[e, 4, z], (gx, below, gz)),
        )

    def field_copies_low(e):
        send, recv = f_send_z, f_recv_z
        return (
            copy(p_first.at[e, 0], x_hi.at[e, PLANES], send.at[e, 0], recv.at[e, 0], (left, gy, other)),
            copy(st.at[e, 1, pl.ds(0, 8)], y_hi.at[e, PLANES], send.at[e, 1], recv.at[e, 1], (gx, below, other)),
            copy(st.at[e, 1], st.at[e, PLANES + 1], send.at[e, 2], recv.at[e, 2], (gx, gy, other)),
        )

    def field_copies_high(e):
        return (
            copy(st.at[e, PLANES], st.at[e, 0], f_send_z.at[e, 3], f_recv_z.at[e, 3], (gx, gy, other)),
        )

    def adjoint_copies(e, z):
        send, recv = b_send, b_recv
        return (
            copy(pa_last.at[e, z], xa.at[e, z + 1], send.at[e, 0, z], recv.at[e, 0, z], (right, gy, gz)),
            copy(pa_first.at[e, z], xb.at[e, z], send.at[e, 1, z], recv.at[e, 1, z], (left, gy, gz)),
            copy(pa_last.at[e, z], xya.at[e, z], send.at[e, 2, z], recv.at[e, 2, z], (right, above, gz)),
            copy(y_tiles.at[e, z], ya.at[e, z + 1], send.at[e, 3, z], recv.at[e, 3, z], (gx, above, gz)),
            copy(q.at[e, z + 1, 4, pl.ds(0, 8)], yb.at[e, z], send.at[e, 4, z], recv.at[e, 4, z], (gx, below, gz)),
        )

    def adjoint_copies_high(e):
        send, recv = b_send_z, b_recv_z
        return (
            copy(pa_last.at[e, PLANES - 1], xa.at[e, 0], send.at[e, 0], recv.at[e, 0], (right, gy, other)),
            copy(y_tiles.at[e, PLANES - 1], ya.at[e, 0], send.at[e, 1], recv.at[e, 1], (gx, above, other)),
            copy(z_up.at[e], q.at[e, 0, 5], send.at[e, 2], recv.at[e, 2], (gx, gy, other)),
        )

    def adjoint_copies_low(e):
        return (
            copy(q.at[e, 1, 6], q.at[e, PLANES + 1, 6], b_send_z.at[e, 3], b_recv_z.at[e, 3], (gx, gy, other)),
        )

    def start(copies):
        for each in copies:
            each.start()

    def arrive(copies):
        for each in copies:
            each.wait_recv()

    def sent(copies):
        for each in copies:
            each.wait_send()

    def send_fields(e, z):
        plane = st[e, z + 1]
        empty = jnp.zeros((8, LANES), f32)
        p_first[e, z] = pack_lane(plane, 0, 0, empty)
        p_last[e, z] = pack_lane(plane, LANES - 1, 0, empty)
        start(field_copies(e, z))

        @pl.when(z == 0)
        def _():
            start(field_copies_low(e))

        @pl.when(z == PLANES - 1)
        def _():
            start(field_copies_high(e))

    def place(step):
        odd = lax.rem(step, 2)
        half = lax.div(step, 2)
        return half + odd * (PLANES - 1 - 2 * half)

    def lay_out(z, carry):
        for k in range(FIELDS):
            st[0, z + 1, pl.ds(k, 16, stride=FIELDS), :] = state_in[k, z]
        return carry

    lax.fori_loop(0, PLANES, lay_out, 0)
    pl.semaphore_wait(barrier, 4 + (group - 1) + (ny - 1))

    def first_sends(step, carry):
        send_fields(0, place(step))
        return carry

    lax.fori_loop(0, PLANES, first_sends, 0)

    def lay_out_rest(z, carry):
        for k in range(FIELDS):
            cot[z, pl.ds(k, 16, stride=FIELDS), :] = cot_in[k, z]
            spread4[z, pl.ds(k, 16, stride=FIELDS), :] = diff_in[z]
        return carry

    lax.fori_loop(0, PLANES, lay_out_rest, 0)
    for e in range(2):
        for j in (8, 9):
            q[e, 0, j] = jnp.zeros((ROWS, LANES), f32)

    zero4 = jnp.zeros((4, LANES), f32)
    first = w_in[...].astype(f32)
    parts = [first[4 * j : 4 * j + 4] for j in range(STENCIL)]
    even = jnp.concatenate([piece for part in parts for piece in (part, zero4)], axis=0)
    odd = jnp.concatenate([piece for part in parts for piece in (zero4, part)], axis=0)
    v_one[...] = jnp.concatenate([even, odd], axis=1).astype(bf16)
    bias_high = biases[...].astype(bf16).astype(f32)
    bias_low = biases[...] - bias_high

    def bias_rows(layer):
        return jnp.concatenate(
            [
                0.5 * bias_high[layer : layer + 1],
                0.5 * bias_low[layer : layer + 1],
                jnp.zeros((14, HID), f32),
            ],
            axis=0,
        )

    def turned_first(half):
        tall = jnp.concatenate([0.5 * half, bias_rows(0), jnp.zeros((32, HID), f32)], axis=0)
        return tall.T[:, :96]

    l_one[...] = jnp.concatenate([turned_first(even), turned_first(odd)], axis=0).astype(bf16)
    for layer, source, ahead, back in ((1, w_second, l_two, v_two), (2, w_third, l_three, v_three)):
        matrix = 0.5 * source[...].astype(f32)
        back[...] = matrix.astype(bf16)
        tall = jnp.concatenate([bias_rows(layer), jnp.zeros((112, HID), f32)], axis=0)
        ahead[...] = jnp.concatenate([matrix.T, tall.T[:, :16]], axis=1).astype(bf16)
    square[...] = jnp.zeros((HID, HID), f32)
    square[:, 0:FIELDS] = w_out[...].astype(f32)
    readout = square[...]
    turned_out = readout.T[0:4]
    zero8 = jnp.zeros((8, LANES), f32)
    l_out[...] = jnp.concatenate(
        [
            jnp.concatenate([turned_out, zero4, zero8], axis=0),
            jnp.concatenate([zero4, turned_out, zero8], axis=0),
        ],
        axis=1,
    ).astype(bf16)
    v_out[...] = jnp.concatenate(
        [0.5 * readout[:, :16], 0.5 * pltpu.roll(readout, FIELDS, 1)[:, :16]], axis=0
    ).astype(bf16)
    field_row = lax.rem(lax.broadcasted_iota(jnp.int32, (8, LANES), 0), FIELDS)
    bias_tile = jnp.zeros((8, LANES), f32)
    for k in range(FIELDS):
        bias_tile = jnp.where(field_row == k, bias_out[k], bias_tile)
    bias_plane = jnp.concatenate([bias_tile] * 8, axis=0)
    for each in (g_one, g_two, g_three, g_four):
        each[...] = jnp.zeros(each.shape, f32)

    lane = lane_index(ROWS)
    lane8 = lane_index(8)
    sub_width = WIDE // SUBS
    ones_rows = lax.broadcasted_iota(jnp.int32, (16, WIDE), 0)
    ones_wide = jnp.where(ones_rows < 2, 1.0, 0.0).astype(bf16)
    ones_cells = jnp.concatenate([ones_wide[:, :sub_width]] * 2, axis=1)

    def to_right(plane, e, z):
        return jnp.where(
            lane == LANES - 1, unpack_lane(x_hi[e, z], 0, LANES - 1), pltpu.roll(plane, LANES - 1, 1)
        )

    def stencil(e, z):
        here, ahead, behind = st[e, z + 1], st[e, z + 2], st[e, z]
        beyond = y_hi[e, z]
        at_right = to_right(here, e, z)
        at_left = jnp.where(lane == 0, unpack_lane(x_lo[e, z], 0, 0), pltpu.roll(here, 1, 1))
        corner = jnp.where(
            lane8 == LANES - 1,
            pltpu.roll(xy_hi[e, z], LANES - 1, 1),
            pltpu.roll(beyond, LANES - 1, 1),
        )
        return (
            here,
            at_right,
            at_left,
            rows_down(here, beyond[0:4]),
            rows_up(here, y_lo[e, z][4:8]),
            ahead,
            behind,
            rows_down(at_right, corner[0:4]),
            rows_down(ahead, y_hi[e, z + 1][0:4]),
            to_right(ahead, e, z + 1),
        )

    def arrange(points):
        rows = jnp.concatenate([wide_of(point) for point in points], axis=0)
        return jnp.concatenate([rows.astype(bf16), ones_wide], axis=0)

    def laplace(points):
        total_of = -6.0 * points[0]
        for point in points[1:7]:
            total_of = total_of + point
        return total_of

    def layers(features):
        value, slope = silu_parts(side_by_side(mm(l_one[...], features)))
        values, doubled = [value], [slope]
        for matrix in (l_two, l_three):
            cells = jnp.concatenate([value, ones_cells], axis=0)
            value, slope = silu_parts(mm(matrix[...], cells))
            values.append(value)
            doubled.append(slope)
        return values, doubled

    def readout_of(value):
        return mm(l_out[...], stacked_of(value))[0:8]

    def times(product, slope):
        return (product * slope.astype(f32)).astype(bf16)

    def grad_rows(adjoint):
        scaled = wide_of(time_step * adjoint)
        return jnp.concatenate([scaled, jnp.zeros((8, WIDE), f32)], axis=0).astype(bf16)

    def backward(features, values, doubled, grad_out):
        back_three = times(side_by_side(mm(v_out[...], grad_out)), doubled[2])
        back_two = times(mm(v_three[...], back_three), doubled[1])
        back_one = stacked_of(times(mm(v_two[...], back_two), doubled[0]))
        ones_here = ones_cells[:, :sub_width]
        g_four[:, 0:16] += mm_cells(
            jnp.concatenate([stacked_of(values[2]), ones_here], axis=0), grad_out
        )
        g_three[...] += mm_cells(jnp.concatenate([values[1], ones_cells], axis=0), back_three)
        g_two[...] += mm_cells(jnp.concatenate([values[0], ones_cells], axis=0), back_two)
        g_one[...] += mm_cells(features, back_one)
        return mm(v_one[...], back_one)

    def send_adjoint(e, z, wide, adjoint):
        spread = spread4[z] * adjoint
        for j in range(STENCIL):
            part = plane_of(wide[8 * j : 8 * j + 8])
            if j == 0:
                part = part - 6.0 * spread
            elif j < 7:
                part = part + spread
            q[e, z + 1, j] = part
        empty = jnp.zeros((8, LANES), f32)
        across = pack_lane(q[e, z + 1, 1], LANES - 1, 0, empty)
        across = pack_lane(q[e, z + 1, 9], LANES - 1, 8, across)
        pa_last[e, z] = pack_lane(q[e, z + 1, 7], LANES - 1, 16, across)
        pa_first[e, z] = pack_lane(q[e, z + 1, 2], 0, 0, empty)
        slanted = q[e, z + 1, 7, 56:64]
        slanted = jnp.where(lane8 == 0, 0.0, pltpu.roll(slanted, 1, 1))
        y_tiles[e, z, 0:8] = q[e, z + 1, 3, 56:64] + slanted
        y_tiles[e, z, 8:16] = q[e, z + 1, 8, 56:64]
        start(adjoint_copies(e, z))

        @pl.when(z == 0)
        def _():
            start(adjoint_copies_low(e))

        @pl.when(z == PLANES - 1)
        def _():
            moved = jnp.where(lane == 0, 0.0, pltpu.roll(q[e, PLANES, 9], 1, 1))
            z_up[e] = q[e, PLANES, 5] + moved + rows_up(q[e, PLANES, 8], zero4)
            start(adjoint_copies_high(e))

    def gather(e, z, adjoint):
        here = z + 1
        result = adjoint + q[e, here, 0] + q[e, z, 5] + q[e, z + 2, 6]
        from_left = q[e, here, 1] + q[e, z, 9] + rows_up(q[e, here, 7], zero4)
        packed = xa[e, here]
        direct = unpack_lane(packed + pltpu.roll(xa[e, z], LANES - 8, 1), 0, 0)
        corner = pltpu.roll(xya[e, z], LANES - 23, 1)[4:8]
        edge = direct + rows_up(unpack_lane(packed, 16, 0), corner)
        result = result + jnp.where(lane == 0, edge, pltpu.roll(from_left, 1, 1))
        result = result + jnp.where(
            lane == LANES - 1,
            unpack_lane(xb[e, z], 0, LANES - 1),
            pltpu.roll(q[e, here, 2], LANES - 1, 1),
        )
        rows_in = ya[e, here, 0:8] + ya[e, z, 8:16]
        result = result + rows_up(q[e, here, 3] + q[e, z, 8], rows_in[4:8])
        return result + rows_down(q[e, here, 4], yb[e, z][0:4])

    def await_fields(e, step):
        @pl.when(step == 0)
        def _():
            arrive(field_copies(e, 0))
            arrive(field_copies(e, 1))
            arrive(field_copies_high(e))

        @pl.when(step == 1)
        def _():
            arrive(field_copies(e, 5))
            arrive(field_copies_low(e))

        @pl.when(step == 2)
        def _():
            arrive(field_copies(e, 2))

        @pl.when(step == 3)
        def _():
            arrive(field_copies(e, 4))

        @pl.when(step == 4)
        def _():
            arrive(field_copies(e, 3))

    def await_adjoint(e, step):
        @pl.when(step == 0)
        def _():
            arrive(adjoint_copies(e, 0))
            arrive(adjoint_copies_high(e))

        @pl.when(step == 1)
        def _():
            arrive(adjoint_copies(e, 5))
            arrive(adjoint_copies(e, 4))
            arrive(adjoint_copies_low(e))

        @pl.when(step == 2)
        def _():
            arrive(adjoint_copies(e, 1))

        @pl.when(step == 3)
        def _():
            arrive(adjoint_copies(e, 3))

        @pl.when(step == 4)
        def _():
            arrive(adjoint_copies(e, 2))

    def piece(sub):
        return slice(sub * sub_width, (sub + 1) * sub_width)

    def beside(sub):
        return slice(2 * sub * sub_width, 2 * (sub + 1) * sub_width)

    def stepped(points, z, wide):
        closed = plane_of(wide) + bias_plane
        return points[0] + spread4[z] * laplace(points) + time_step * closed

    def put(target, z, plane):
        staged[...] = plane
        for k in range(FIELDS):
            target[k, z] = staged[pl.ds(k, 16, stride=FIELDS), :]

    def first_step(step, carry):
        z = place(step)
        await_fields(0, step)
        points = stencil(0, z)
        features = arrange(points)
        feats[z] = features
        outs = []
        for sub in range(SUBS):
            values, doubled = layers(features[:, piece(sub)])
            for layer in range(3):
                acts[layer, z, :, beside(sub)] = values[layer]
                slopes[layer, z, :, beside(sub)] = doubled[layer]
            outs.append(readout_of(values[2]))
        st[1, z + 1] = stepped(points, z, jnp.concatenate(outs, axis=1))
        send_fields(1, z)
        return carry

    lax.fori_loop(0, PLANES, first_step, 0)

    def second_step(step, carry):
        z = place(step)
        await_fields(1, step)
        points = stencil(1, z)
        features = arrange(points)
        adjoint = cot[z]
        grad_out = grad_rows(adjoint)
        outs, wides = [], []
        for sub in range(SUBS):
            values, doubled = layers(features[:, piece(sub)])
            outs.append(readout_of(values[2]))
            wides.append(
                backward(features[:, piece(sub)], values, doubled, grad_out[:, piece(sub)])
            )
        put(final_out, z, stepped(points, z, jnp.concatenate(outs, axis=1)))
        send_adjoint(0, z, jnp.concatenate(wides, axis=1), adjoint)
        return carry

    lax.fori_loop(0, PLANES, second_step, 0)

    def first_back(step, carry):
        z = place(step)
        await_adjoint(0, step)
        adjoint = gather(0, z, cot[z])
        adj_mid[z] = adjoint
        grad_out = grad_rows(adjoint)
        wides = []
        for sub in range(SUBS):
            values = [acts[layer, z, :, beside(sub)] for layer in range(3)]
            doubled = [slopes[layer, z, :, beside(sub)] for layer in range(3)]
            wides.append(
                backward(feats[z, :, piece(sub)], values, doubled, grad_out[:, piece(sub)])
            )
        send_adjoint(1, z, jnp.concatenate(wides, axis=1), adjoint)
        return carry

    lax.fori_loop(0, PLANES, first_back, 0)

    one = g_one[...]
    merged = one[:, :HID] + jnp.concatenate([one[4:, HID:], one[:4, HID:]], axis=0)
    first_rows = jnp.concatenate([merged[8 * j : 8 * j + 4] for j in range(STENCIL)], axis=0)
    four = g_four[...]
    shifted = four[:HID] + pltpu.roll(four[HID : 2 * HID], LANES - FIELDS, 1)
    last = four[2 * HID : 2 * HID + 8]
    last = last + pltpu.roll(last, LANES - FIELDS, 1)
    rest = jnp.concatenate(
        [
            one[80:81, :HID] + one[80:81, HID:],
            g_two[HID : HID + 1],
            g_three[HID : HID + 1],
            last[0:1],
            shifted.T[0:4],
        ],
        axis=0,
    )
    everything = jnp.concatenate(
        [
            g_two[0:HID],
            g_three[0:HID],
            first_rows,
            rest,
            jnp.zeros((SUMS - 304, LANES), f32),
        ],
        axis=0,
    )
    sums[...] = everything.reshape(group, share, LANES)

    def scatter(step):
        target = lax.rem(mine + step, group)
        return copy(sums.at[target], landed_a.at[step], a_send.at[0, step], a_recv.at[0, step], member(target))

    def across(step):
        target = lax.rem(gy + step, ny)
        return copy(landed_b.at[gy], landed_b.at[gy], a_send.at[1, step], a_recv.at[1, gy], (gx, target, gz))

    def across_in(step):
        source = lax.rem(gy + ny - step, ny)
        return copy(landed_b.at[source], landed_b.at[source], a_send.at[1, step], a_recv.at[1, source], (gx, source, gz))

    def spread_out(step):
        target = lax.rem(mine + step, group)
        return copy(total.at[mine], total.at[mine], a_send.at[2, step], a_recv.at[2, mine], member(target))

    def spread_in(step):
        source = lax.rem(mine + group - step, group)
        return copy(total.at[source], total.at[source], a_send.at[2, step], a_recv.at[2, source], member(source))

    def each(count, act):
        def body(step, carry):
            act(step)
            return carry

        lax.fori_loop(1, count, body, 0)

    each(group, lambda step: scatter(step).start())

    def last_gather(step, carry):
        z = place(step)
        await_adjoint(1, step)
        put(adjoint_out, z, gather(1, z, adj_mid[z]))
        return carry

    each(group, lambda step: scatter(step).wait_recv())
    held = sums[mine]
    for step in range(1, group):
        held = held + landed_a[step]
    landed_b[gy] = held
    each(ny, lambda step: across(step).start())

    lax.fori_loop(0, PLANES, last_gather, 0)

    each(ny, lambda step: across_in(step).wait_recv())
    held = landed_b[0]
    for step in range(1, ny):
        held = held + landed_b[step]
    total[mine] = held * scale
    each(group, lambda step: spread_out(step).start())

    def finish_sends(z, carry):
        for e in range(2):
            sent(field_copies(e, z))
            sent(adjoint_copies(e, z))
        return carry

    lax.fori_loop(0, PLANES, finish_sends, 0)
    for e in range(2):
        sent(field_copies_low(e))
        sent(field_copies_high(e))
        sent(adjoint_copies_low(e))
        sent(adjoint_copies_high(e))
    each(group, lambda step: scatter(step).wait_send())
    each(ny, lambda step: across(step).wait_send())
    each(group, lambda step: spread_in(step).wait_recv())

    whole = total[...].reshape(SUMS, LANES)
    g_second_out[...] = whole[0:HID]
    g_third_out[...] = whole[HID : 2 * HID]
    g_in_out[...] = whole[2 * HID : 2 * HID + 40]
    tail = whole[296:304]
    g_biases_out[...] = tail[0:3]
    tall = jnp.concatenate([tail[4:8], jnp.zeros((HID - 4, LANES), f32)], axis=0)
    g_readout_out[...] = tall.T[:, 0:FIELDS]
    g_bias_out_out[...] = tail[3:4, 0:FIELDS]
    each(group, lambda step: spread_out(step).wait_send())


def solution(mesh):
    sizes = (mesh.shape["gx"], mesh.shape["gy"], mesh.shape["gz"])
    nx, ny, nz = sizes
    group = nx * nz
    share = SUMS // group
    cells = PLANES * 16 * LANES * nx * ny * nz
    scale = 1.0 / (time_step * math.sqrt(float(cells)))
    vmem = pl.BlockSpec(memory_space=pltpu.VMEM)
    block = jax.ShapeDtypeStruct((FIELDS, PLANES, 16, LANES), f32)
    tile = (8, LANES)
    dma = pltpu.SemaphoreType.DMA

    def buffer(*shape):
        return pltpu.VMEM(shape, f32)

    def packed(*shape):
        return pltpu.VMEM(shape, bf16)

    scratch = [
        buffer(2, PLANES + 2, ROWS, LANES),
        buffer(2, PLANES, *tile),
        buffer(2, PLANES, *tile),
        buffer(2, PLANES, *tile),
        buffer(2, PLANES + 1, *tile),
        buffer(2, PLANES, *tile),
        buffer(2, PLANES, *tile),
        buffer(2, PLANES + 1, *tile),
        buffer(PLANES, ROWS, LANES),
        buffer(PLANES, ROWS, LANES),
        buffer(PLANES, ROWS, LANES),
        buffer(ROWS, LANES),
        packed(PLANES, 96, WIDE),
        packed(3, PLANES, HID, 2 * WIDE),
        packed(3, PLANES, HID, 2 * WIDE),
        buffer(2, PLANES + 2, STENCIL, ROWS, LANES),
        buffer(2, PLANES, *tile),
        buffer(2, PLANES, *tile),
        buffer(2, PLANES, 16, LANES),
        buffer(2, ROWS, LANES),
        buffer(2, PLANES + 1, *tile),
        buffer(2, PLANES, *tile),
        buffer(2, PLANES, *tile),
        buffer(2, PLANES + 1, 16, LANES),
        buffer(2, PLANES, *tile),
        packed(2 * HID, 96),
        packed(HID, 144),
        packed(HID, 144),
        packed(16, 2 * HID),
        packed(2 * HID, 16),
        packed(HID, HID),
        packed(HID, HID),
        packed(80, 2 * HID),
        buffer(HID, HID),
        buffer(96, 2 * HID),
        buffer(144, HID),
        buffer(144, HID),
        buffer(2 * HID + 16, LANES),
        buffer(group, share, LANES),
        buffer(group, share, LANES),
        buffer(ny, share, LANES),
        buffer(group, share, LANES),
        dma((2, 5, PLANES)),
        dma((2, 5, PLANES)),
        dma((2, 4)),
        dma((2, 4)),
        dma((2, 5, PLANES)),
        dma((2, 5, PLANES)),
        dma((2, 4)),
        dma((2, 4)),
        dma((3, max(group, ny))),
        dma((3, max(group, ny))),
    ]

    def on_device(*operands):
        outs = pl.pallas_call(
            functools.partial(kernel, sizes, scale),
            out_shape=(
                block,
                block,
                jax.ShapeDtypeStruct((40, HID), f32),
                jax.ShapeDtypeStruct((HID, HID), f32),
                jax.ShapeDtypeStruct((HID, HID), f32),
                jax.ShapeDtypeStruct((HID, FIELDS), f32),
                jax.ShapeDtypeStruct((3, HID), f32),
                jax.ShapeDtypeStruct((1, FIELDS), f32),
            ),
            in_specs=[vmem] * 8 + [pl.BlockSpec(memory_space=pltpu.SMEM)],
            out_specs=[vmem] * 8,
            scratch_shapes=scratch,
            compiler_params=pltpu.CompilerParams(
                collective_id=0, has_side_effects=True, vmem_limit_bytes=60 * 2**20
            ),
            name="two_steps_and_adjoint",
        )(*operands)
        return outs[:7] + (outs[7].reshape(FIELDS),)

    fields = P(None, "gz", "gy", "gx")
    placed = (fields, fields, P("gz", "gy", "gx")) + (P(),) * 6
    return jax.shard_map(
        on_device,
        mesh=mesh,
        in_specs=placed,
        out_specs=(fields, fields) + (P(),) * 6,
        check_vma=False,
    )
```

time: 892 us -> 88.3 us (0.10); the launches traced: 881 us -> 88 us
  local copies, waits for them, and re-layouts: 308 us -> 8.6 us
  waiting for transfers between devices: 253 us -> 0 us
  matrix products: 111 us -> 0 us
  blocking collectives: 80 us -> 0 us
  Pallas kernels: 0 us -> 78.7 us
  other arithmetic: 66.8 us -> 0 us
  starting transfers between devices: 45.5 us -> 0 us
  between operations: 15.6 us -> 0.65 us
    scatter-add x42 -> x0, local copies, waits for them, and re-layouts: 249 us -> none  [the longest x32 232 us: retreat(): buffer = buffer.at[:, 1 + offset[0]:1 + offset[0] + extent[0], 1 + offset...]
    psum x1 -> x0, waiting for transfers between devices: 238 us -> none  [on_device(): lax.psum((local_grads[0], local_grads[1], local_grads[2], local_grads[3],...]
    dot_general x156 -> x0, matrix products: 111 us -> none  [the longest x60 60.7 us: contract(): lax.dot_general(former, latter, (((0,), (0,)), ((), ())), preferred_eleme...]
    psum x1 -> x0, blocking collectives: 80 us -> none  [on_device(): lax.psum((local_grads[0], local_grads[1], local_grads[2], local_grads[3],...]
    pallas_call x0 -> x1, Pallas kernels: none -> 78.7 us  [on_device(): pl.pallas_call(functools.partial(kernel, sizes, scale), out_shape=(block,...]
    ppermute x24 -> x0, starting transfers between devices: 45.5 us -> none  [the longest x12 32.1 us: extended(): lax.ppermute(lax.slice_in_dim(block, 0, width, axis=dim), axis, backward)]
    add x72 -> x0, other arithmetic: 40.5 us -> none  [the longest x32 20.5 us: retreat(): buffer = buffer.at[:, 1 + offset[0]:1 + offset[0] + extent[0], 1 + offset...]
    another operation x28 -> x0, local copies, waits for them, and re-layouts: 29.6 us -> none
  transfers between devices with their start and end apart: 25 -> 0, of which waited for: 8 -> 0; matrix products, arithmetic and copies ran while one was open for 11% -> 0% of each run, Pallas kernels for 0% -> 0%
where the time goes in v1:
time: 88.3 us; the launch traced here: 88 us
  Pallas kernels  78.7 us (89%)
  local copies, waits for them, and re-layouts  8.6 us (10%)
    pallas_call x1, Pallas kernels, on_device(): pl.pallas_call(functools.partial(kernel, sizes, scale), out_shape=(block,...  78.7 us
    unnamed x21, local copies, waits for them, and re-layouts  8.6 us

profile of v1, /device:TPU:1, one launch (start us, length us, event | category | flops | bytes accessed | tf_op | source)
XLA Modules:
  0.0 88.0 jit_solution(3568193080234988024)
XLA Ops:
  0.6 1.4 %copy.17.w_out = bf16[128,4]{1,0:T(8,128)(2,1)} copy(bf16[128,4]{0,1:T(4,128)(2,1)} %param.15) | data formatting | bytes 2048 | tf_op args[6]
  2.0 78.7 %two_steps_and_adjoint.1 = (f32[4,6,16,128]{3,2,1,0:T(8,128)}, f32[4,6,16,128]{3,2,1,0:T(8,128)}, f32[40,128]{1,0:T(8,128)}, f32[128,128]{1,0:T(8,128)}, f32[128...) custom-call(f32[4,6,16,128]{3,2,1,0:T(8,128)} %state_in.1, f32[4,6,16,128]{3,2,1,0:T(8,128)} %cot_in.1, ...), custom_call_target="tpu_custom_call" | custom-call | tf_op jit(solution)/shard_map/two_steps_and_adjoint/pallas_call | solution.py:786
  80.8 1.5 %copy.18 = f32[128,4]{0,1:T(4,128)} copy(f32[128,4]{1,0:T(8,128)} %get-tuple-element.29) | data formatting | bytes 4096
  82.3 0.0 copy-start
  82.3 1.7 %copy.26 = f32[4,6,16,128]{3,2,1,0:T(8,128)} copy(f32[4,6,16,128]{3,2,1,0:T(8,128)} %get-tuple-element.40) | data formatting | bytes 393216
  83.9 0.0 copy-done
  83.9 0.0 copy-start.3
  83.9 0.0 copy-start.2
  83.9 0.7 copy.27
  84.6 0.0 copy-done.3
  84.7 0.6 copy.28
  85.3 0.0 copy-done.2
  85.3 0.0 copy-start.1
  85.3 0.6 copy.29
  85.9 0.2 copy-done.1
  86.1 0.0 copy-start.4
  86.1 0.6 copy.30
  86.8 0.0 copy-done.4
  86.8 0.0 copy-start.5
  86.8 0.6 copy.31
  87.4 0.1 copy-done.5
  87.5 0.5 copy.32
Async XLA Ops:
  82.3 1.7 %copy-start = (f32[4,6,16,128]{3,2,1,0:T(8,128)S(1)}, f32[4,6,16,128]{3,2,1,0:T(8,128)}, u32[]{:S(2)}) copy-start(f32[4,6,16,128]{3,2,1,0:T(8,128)} %get-tuple-element.41) | copy-start | bytes 589828
  83.9 0.7 copy-start.3
  83.9 1.3 %copy-start.2 = (f32[128,128]{1,0:T(8,128)S(1)}, f32[128,128]{1,0:T(8,128)}, u32[]{:S(2)}) copy-start(f32[128,128]{1,0:T(8,128)} %get-tuple-element.43) | copy-start | bytes 196612
  85.3 0.9 copy-start.1
  86.1 0.7 copy-start.4
  86.8 0.7 copy-start.5

commit v2 on v1

--- a/solution.py
+++ b/solution.py
@@ -78,11 +78,12 @@
 
 
 def silu_parts(half):
+    half = half.astype(bf16)
     turned = jnp.tanh(half)
-    raised = 1.0 + turned
+    raised = 1 + turned
     value = half * raised
-    slope = raised * (1.0 - half * turned) + value
-    return value.astype(bf16), slope.astype(bf16)
+    slope = raised * (1 - half * turned) + value
+    return value, slope
 
 
 def kernel(
@@ -105,6 +106,16 @@
     g_readout_out,
     g_biases_out,
     g_bias_out_out,
+    state_here,
+    cot_here,
+    diff_here,
+    w_in_here,
+    w_second_here,
+    w_third_here,
+    w_out_here,
+    biases_here,
+    final_here,
+    adjoint_here,
     st,
     p_first,
     p_last,
@@ -120,6 +131,7 @@
     feats,
     acts,
     slopes,
+    backs,
     q,
     pa_last,
     pa_first,
@@ -138,12 +150,12 @@
     v_three,
     v_two,
     v_one,
-    square,
     g_one,
     g_two,
     g_three,
     g_four,
     sums,
+    landed_pair,
     landed_a,
     landed_b,
     total,
@@ -157,38 +169,60 @@
     b_recv_z,
     a_send,
     a_recv,
+    here_sem,
 ):
     nx, ny, nz = sizes
     gx, gy, gz = lax.axis_index("gx"), lax.axis_index("gy"), lax.axis_index("gz")
     right, left = lax.rem(gx + 1, nx), lax.rem(gx + nx - 1, nx)
     above, below = lax.rem(gy + 1, ny), lax.rem(gy + ny - 1, ny)
     other = 1 - gz
-    group = nx * nz
-    mine = gx * nz + gz
-    share = SUMS // group
-
-    def member(place):
-        return (lax.div(place, nz), gy, lax.rem(place, nz))
+    share = SUMS // nz // nx
 
     barrier = pltpu.get_barrier_semaphore()
 
     def greet(device):
         pl.semaphore_signal(barrier, inc=1, device_id=device, device_id_type=MESH)
 
-    for device in ((right, above, gz), (left, below, gz), (gx, above, other), (gx, below, other)):
+    for device in (
+        (right, above, gz),
+        (left, below, gz),
+        (gx, above, other),
+        (gx, below, other),
+        (right, gy, other),
+        (left, gy, other),
+        (gx, gy, other),
+    ):
         greet(device)
 
-    def greet_group(step, carry):
-        greet(member(lax.rem(mine + step, group)))
-        return carry
-
-    lax.fori_loop(1, group, greet_group, 0)
+    def greet_row(step, carry):
+        greet((lax.rem(gx + step, nx), gy, gz))
+        return carry
+
+    lax.fori_loop(1, nx, greet_row, 0)
 
     def greet_column(step, carry):
         greet((gx, lax.rem(gy + step, ny), gz))
         return carry
 
     lax.fori_loop(1, ny, greet_column, 0)
+
+    fetches = [
+        pltpu.make_async_copy(source, target, here_sem.at[number])
+        for number, (source, target) in enumerate(
+            (
+                (state_in, state_here),
+                (cot_in, cot_here),
+                (diff_in, diff_here),
+                (w_in, w_in_here),
+                (w_second, w_second_here),
+                (w_third, w_third_here),
+                (w_out, w_out_here),
+                (biases, biases_here),
+            )
+        )
+    ]
+    for fetch in fetches:
+        fetch.start()
 
     def copy(source, target, send, recv, device):
         return pltpu.make_async_remote_copy(
@@ -280,11 +314,12 @@
 
     def lay_out(z, carry):
         for k in range(FIELDS):
-            st[0, z + 1, pl.ds(k, 16, stride=FIELDS), :] = state_in[k, z]
-        return carry
-
+            st[0, z + 1, pl.ds(k, 16, stride=FIELDS), :] = state_here[k, z]
+        return carry
+
+    fetches[0].wait()
     lax.fori_loop(0, PLANES, lay_out, 0)
-    pl.semaphore_wait(barrier, 4 + (group - 1) + (ny - 1))
+    pl.semaphore_wait(barrier, 7 + (nx - 1) + (ny - 1))
 
     def first_sends(step, carry):
         send_fields(0, place(step))
@@ -292,10 +327,13 @@
 
     lax.fori_loop(0, PLANES, first_sends, 0)
 
+    for fetch in fetches[1:]:
+        fetch.wait()
+
     def lay_out_rest(z, carry):
         for k in range(FIELDS):
-            cot[z, pl.ds(k, 16, stride=FIELDS), :] = cot_in[k, z]
-            spread4[z, pl.ds(k, 16, stride=FIELDS), :] = diff_in[z]
+            cot[z, pl.ds(k, 16, stride=FIELDS), :] = cot_here[k, z]
+            spread4[z, pl.ds(k, 16, stride=FIELDS), :] = diff_here[z]
         return carry
 
     lax.fori_loop(0, PLANES, lay_out_rest, 0)
@@ -304,13 +342,13 @@
             q[e, 0, j] = jnp.zeros((ROWS, LANES), f32)
 
     zero4 = jnp.zeros((4, LANES), f32)
-    first = w_in[...].astype(f32)
+    first = w_in_here[...].astype(f32)
     parts = [first[4 * j : 4 * j + 4] for j in range(STENCIL)]
     even = jnp.concatenate([piece for part in parts for piece in (part, zero4)], axis=0)
     odd = jnp.concatenate([piece for part in parts for piece in (zero4, part)], axis=0)
     v_one[...] = jnp.concatenate([even, odd], axis=1).astype(bf16)
-    bias_high = biases[...].astype(bf16).astype(f32)
-    bias_low = biases[...] - bias_high
+    bias_high = biases_here[...].astype(bf16).astype(f32)
+    bias_low = biases_here[...] - bias_high
 
     def bias_rows(layer):
         return jnp.concatenate(
@@ -327,15 +365,16 @@
         return tall.T[:, :96]
 
     l_one[...] = jnp.concatenate([turned_first(even), turned_first(odd)], axis=0).astype(bf16)
-    for layer, source, ahead, back in ((1, w_second, l_two, v_two), (2, w_third, l_three, v_three)):
+    for layer, source, ahead, back in (
+        (1, w_second_here, l_two, v_two),
+        (2, w_third_here, l_three, v_three),
+    ):
         matrix = 0.5 * source[...].astype(f32)
         back[...] = matrix.astype(bf16)
         tall = jnp.concatenate([bias_rows(layer), jnp.zeros((112, HID), f32)], axis=0)
         ahead[...] = jnp.concatenate([matrix.T, tall.T[:, :16]], axis=1).astype(bf16)
-    square[...] = jnp.zeros((HID, HID), f32)
-    square[:, 0:FIELDS] = w_out[...].astype(f32)
-    readout = square[...]
-    turned_out = readout.T[0:4]
+    turned_out = w_out_here[...].astype(f32)
+    readout = jnp.concatenate([turned_out, jnp.zeros((HID - FIELDS, HID), f32)], axis=0).T
     zero8 = jnp.zeros((8, LANES), f32)
     l_out[...] = jnp.concatenate(
         [
@@ -400,38 +439,57 @@
             total_of = total_of + point
         return total_of
 
-    def layers(features):
+    def layers(features, values, doubled):
         value, slope = silu_parts(side_by_side(mm(l_one[...], features)))
-        values, doubled = [value], [slope]
+        values.append(value)
+        doubled.append(slope)
+        yield
         for matrix in (l_two, l_three):
             cells = jnp.concatenate([value, ones_cells], axis=0)
             value, slope = silu_parts(mm(matrix[...], cells))
             values.append(value)
             doubled.append(slope)
-        return values, doubled
+            yield
 
     def readout_of(value):
         return mm(l_out[...], stacked_of(value))[0:8]
 
     def times(product, slope):
-        return (product * slope.astype(f32)).astype(bf16)
+        return product.astype(bf16) * slope
 
     def grad_rows(adjoint):
         scaled = wide_of(time_step * adjoint)
         return jnp.concatenate([scaled, jnp.zeros((8, WIDE), f32)], axis=0).astype(bf16)
 
     def backward(features, values, doubled, grad_out):
+        ones_here = ones_cells[:, :sub_width]
         back_three = times(side_by_side(mm(v_out[...], grad_out)), doubled[2])
+        yield
         back_two = times(mm(v_three[...], back_three), doubled[1])
-        back_one = stacked_of(times(mm(v_two[...], back_two), doubled[0]))
-        ones_here = ones_cells[:, :sub_width]
+        yield
         g_four[:, 0:16] += mm_cells(
             jnp.concatenate([stacked_of(values[2]), ones_here], axis=0), grad_out
         )
+        back_one = stacked_of(times(mm(v_two[...], back_two), doubled[0]))
+        yield
         g_three[...] += mm_cells(jnp.concatenate([values[1], ones_cells], axis=0), back_three)
+        yield
         g_two[...] += mm_cells(jnp.concatenate([values[0], ones_cells], axis=0), back_two)
+        yield
         g_one[...] += mm_cells(features, back_one)
-        return mm(v_one[...], back_one)
+        return back_one
+
+    def in_turn(pieces):
+        results = [None] * len(pieces)
+        running = list(range(len(pieces)))
+        while running:
+            for number in list(running):
+                try:
+                    next(pieces[number])
+                except StopIteration as end:
+                    results[number] = end.value
+                    running.remove(number)
+        return results
 
     def send_adjoint(e, z, wide, adjoint):
         spread = spread4[z] * adjoint
@@ -550,13 +608,16 @@
         points = stencil(0, z)
         features = arrange(points)
         feats[z] = features
-        outs = []
-        for sub in range(SUBS):
-            values, doubled = layers(features[:, piece(sub)])
-            for layer in range(3):
+
+        def forward(sub):
+            values, doubled = [], []
+            for layer, _ in enumerate(layers(features[:, piece(sub)], values, doubled)):
                 acts[layer, z, :, beside(sub)] = values[layer]
                 slopes[layer, z, :, beside(sub)] = doubled[layer]
-            outs.append(readout_of(values[2]))
+                yield
+            return readout_of(values[2])
+
+        outs = in_turn([forward(sub) for sub in range(SUBS)])
         st[1, z + 1] = stepped(points, z, jnp.concatenate(outs, axis=1))
         send_fields(1, z)
         return carry
@@ -570,18 +631,24 @@
         features = arrange(points)
         adjoint = cot[z]
         grad_out = grad_rows(adjoint)
-        outs, wides = [], []
-        for sub in range(SUBS):
-            values, doubled = layers(features[:, piece(sub)])
-            outs.append(readout_of(values[2]))
-            wides.append(
-                backward(features[:, piece(sub)], values, doubled, grad_out[:, piece(sub)])
+
+        def both_ways(sub):
+            values, doubled = [], []
+            yield from layers(features[:, piece(sub)], values, doubled)
+            out = readout_of(values[2])
+            back_one = yield from backward(
+                features[:, piece(sub)], values, doubled, grad_out[:, piece(sub)]
             )
-        put(final_out, z, stepped(points, z, jnp.concatenate(outs, axis=1)))
+            return out, mm(v_one[...], back_one)
+
+        outs, wides = zip(*in_turn([both_ways(sub) for sub in range(SUBS)]))
+        put(final_here, z, stepped(points, z, jnp.concatenate(outs, axis=1)))
         send_adjoint(0, z, jnp.concatenate(wides, axis=1), adjoint)
         return carry
 
     lax.fori_loop(0, PLANES, second_step, 0)
+    final_copy = pltpu.make_async_copy(final_here, final_out, here_sem.at[8])
+    final_copy.start()
 
     def first_back(step, carry):
         z = place(step)
@@ -589,14 +656,14 @@
         adjoint = gather(0, z, cot[z])
         adj_mid[z] = adjoint
         grad_out = grad_rows(adjoint)
-        wides = []
-        for sub in range(SUBS):
+
+        def back(sub):
             values = [acts[layer, z, :, beside(sub)] for layer in range(3)]
             doubled = [slopes[layer, z, :, beside(sub)] for layer in range(3)]
-            wides.append(
-                backward(feats[z, :, piece(sub)], values, doubled, grad_out[:, piece(sub)])
-            )
-        send_adjoint(1, z, jnp.concatenate(wides, axis=1), adjoint)
+            return backward(feats[z, :, piece(sub)], values, doubled, grad_out[:, piece(sub)])
+
+        for sub, back_one in enumerate(in_turn([back(sub) for sub in range(SUBS)])):
+            backs[z, :, piece(sub)] = back_one
         return carry
 
     lax.fori_loop(0, PLANES, first_back, 0)
@@ -628,58 +695,82 @@
         ],
         axis=0,
     )
-    sums[...] = everything.reshape(group, share, LANES)
+    sums[...] = everything.reshape(nz, nx, share, LANES)
+
+    pair = copy(sums.at[other], landed_pair, a_send.at[0, 0], a_recv.at[0, 0], (gx, gy, other))
 
     def scatter(step):
-        target = lax.rem(mine + step, group)
-        return copy(sums.at[target], landed_a.at[step], a_send.at[0, step], a_recv.at[0, step], member(target))
+        target = lax.rem(gx + step, nx)
+        return copy(
+            sums.at[gz, target], landed_a.at[step], a_send.at[1, step], a_recv.at[1, step], (target, gy, gz)
+        )
 
     def across(step):
         target = lax.rem(gy + step, ny)
-        return copy(landed_b.at[gy], landed_b.at[gy], a_send.at[1, step], a_recv.at[1, gy], (gx, target, gz))
+        return copy(landed_b.at[gy], landed_b.at[gy], a_send.at[2, step], a_recv.at[2, gy], (gx, target, gz))
 
     def across_in(step):
         source = lax.rem(gy + ny - step, ny)
-        return copy(landed_b.at[source], landed_b.at[source], a_send.at[1, step], a_recv.at[1, source], (gx, source, gz))
+        return copy(landed_b.at[source], landed_b.at[source], a_send.at[2, step], a_recv.at[2, source], (gx, source, gz))
 
     def spread_out(step):
-        target = lax.rem(mine + step, group)
-        return copy(total.at[mine], total.at[mine], a_send.at[2, step], a_recv.at[2, mine], member(target))
+        target = lax.rem(gx + step, nx)
+        return copy(total.at[gz, gx], total.at[gz, gx], a_send.at[3, step], a_recv.at[3, gx], (target, gy, gz))
 
     def spread_in(step):
-        source = lax.rem(mine + group - step, group)
-        return copy(total.at[source], total.at[source], a_send.at[2, step], a_recv.at[2, source], member(source))
-
-    def each(count, act):
+        source = lax.rem(gx + nx - step, nx)
+        return copy(total.at[gz, source], total.at[gz, source], a_send.at[3, step], a_recv.at[3, source], (source, gy, gz))
+
+    def hand_over(step):
+        source = lax.rem(gx + nx - step, nx)
+        return copy(total.at[gz, source], total.at[gz, source], a_send.at[4, step], a_recv.at[4, source], (gx, gy, other))
+
+    def hand_over_in(step):
+        source = lax.rem(gx + nx - step, nx)
+        return copy(total.at[other, source], total.at[other, source], a_send.at[4, step], a_recv.at[4, source], (gx, gy, other))
+
+    def each(first, count, act):
         def body(step, carry):
             act(step)
             return carry
 
-        lax.fori_loop(1, count, body, 0)
-
-    each(group, lambda step: scatter(step).start())
+        lax.fori_loop(first, count, body, 0)
+
+    def last_contributions(step, carry):
+        z = place(step)
+        send_adjoint(1, z, mm(v_one[...], backs[z]), adj_mid[z])
+        return carry
 
     def last_gather(step, carry):
         z = place(step)
         await_adjoint(1, step)
-        put(adjoint_out, z, gather(1, z, adj_mid[z]))
-        return carry
-
-    each(group, lambda step: scatter(step).wait_recv())
-    held = sums[mine]
-    for step in range(1, group):
+        put(adjoint_here, z, gather(1, z, adj_mid[z]))
+        return carry
+
+    pair.start()
+    lax.fori_loop(0, 2, last_contributions, 0)
+    pair.wait_recv()
+    sums[gz] = sums[gz] + landed_pair[...]
+    each(1, nx, lambda step: scatter(step).start())
+    lax.fori_loop(2, PLANES, last_contributions, 0)
+    each(1, nx, lambda step: scatter(step).wait_recv())
+    held = sums[gz, gx]
+    for step in range(1, nx):
         held = held + landed_a[step]
     landed_b[gy] = held
-    each(ny, lambda step: across(step).start())
+    each(1, ny, lambda step: across(step).start())
 
     lax.fori_loop(0, PLANES, last_gather, 0)
-
-    each(ny, lambda step: across_in(step).wait_recv())
+    adjoint_copy = pltpu.make_async_copy(adjoint_here, adjoint_out, here_sem.at[9])
+    adjoint_copy.start()
+
+    each(1, ny, lambda step: across_in(step).wait_recv())
     held = landed_b[0]
     for step in range(1, ny):
         held = held + landed_b[step]
-    total[mine] = held * scale
-    each(group, lambda step: spread_out(step).start())
+    total[gz, gx] = held * scale
+    each(1, nx, lambda step: spread_out(step).start())
+    hand_over(0).start()
 
     def finish_sends(z, carry):
         for e in range(2):
@@ -693,9 +784,18 @@
         sent(field_copies_high(e))
         sent(adjoint_copies_low(e))
         sent(adjoint_copies_high(e))
-    each(group, lambda step: scatter(step).wait_send())
-    each(ny, lambda step: across(step).wait_send())
-    each(group, lambda step: spread_in(step).wait_recv())
+    pair.wait_send()
+    each(1, nx, lambda step: scatter(step).wait_send())
+    each(1, ny, lambda step: across(step).wait_send())
+    final_copy.wait()
+    adjoint_copy.wait()
+
+    def pass_on(step):
+        spread_in(step).wait_recv()
+        hand_over(step).start()
+
+    each(1, nx, pass_on)
+    each(0, nx, lambda step: hand_over_in(step).wait_recv())
 
     whole = total[...].reshape(SUMS, LANES)
     g_second_out[...] = whole[0:HID]
@@ -703,17 +803,28 @@
     g_in_out[...] = whole[2 * HID : 2 * HID + 40]
     tail = whole[296:304]
     g_biases_out[...] = tail[0:3]
-    tall = jnp.concatenate([tail[4:8], jnp.zeros((HID - 4, LANES), f32)], axis=0)
-    g_readout_out[...] = tall.T[:, 0:FIELDS]
+    g_readout_out[...] = tail[4:8]
     g_bias_out_out[...] = tail[3:4, 0:FIELDS]
-    each(group, lambda step: spread_out(step).wait_send())
+    each(1, nx, lambda step: spread_out(step).wait_send())
+    each(0, nx, lambda step: hand_over(step).wait_send())
+
+
+def deliver(*refs):
+    count = (len(refs) - 1) // 2
+    copies = [
+        pltpu.make_async_copy(refs[number], refs[count + number], refs[-1].at[number])
+        for number in range(count)
+    ]
+    for each in copies:
+        each.start()
+    for each in copies:
+        each.wait()
 
 
 def solution(mesh):
     sizes = (mesh.shape["gx"], mesh.shape["gy"], mesh.shape["gz"])
     nx, ny, nz = sizes
-    group = nx * nz
-    share = SUMS // group
+    share = SUMS // nz // nx
     cells = PLANES * 16 * LANES * nx * ny * nz
     scale = 1.0 / (time_step * math.sqrt(float(cells)))
     vmem = pl.BlockSpec(memory_space=pltpu.VMEM)
@@ -728,6 +839,16 @@
         return pltpu.VMEM(shape, bf16)
 
     scratch = [
+        buffer(FIELDS, PLANES, 16, LANES),
+        buffer(FIELDS, PLANES, 16, LANES),
+        buffer(PLANES, 16, LANES),
+        packed(40, HID),
+        packed(HID, HID),
+        packed(HID, HID),
+        packed(FIELDS, HID),
+        buffer(3, HID),
+        buffer(FIELDS, PLANES, 16, LANES),
+        buffer(FIELDS, PLANES, 16, LANES),
         buffer(2, PLANES + 2, ROWS, LANES),
         buffer(2, PLANES, *tile),
         buffer(2, PLANES, *tile),
@@ -743,6 +864,7 @@
         packed(PLANES, 96, WIDE),
         packed(3, PLANES, HID, 2 * WIDE),
         packed(3, PLANES, HID, 2 * WIDE),
+        packed(PLANES, 2 * HID, WIDE),
         buffer(2, PLANES + 2, STENCIL, ROWS, LANES),
         buffer(2, PLANES, *tile),
         buffer(2, PLANES, *tile),
@@ -761,15 +883,15 @@
         packed(HID, HID),
         packed(HID, HID),
         packed(80, 2 * HID),
-        buffer(HID, HID),
         buffer(96, 2 * HID),
         buffer(144, HID),
         buffer(144, HID),
         buffer(2 * HID + 16, LANES),
-        buffer(group, share, LANES),
-        buffer(group, share, LANES),
+        buffer(nz, nx, share, LANES),
+        buffer(nx, share, LANES),
+        buffer(nx, share, LANES),
         buffer(ny, share, LANES),
-        buffer(group, share, LANES),
+        buffer(nz, nx, share, LANES),
         dma((2, 5, PLANES)),
         dma((2, 5, PLANES)),
         dma((2, 4)),
@@ -778,32 +900,45 @@
         dma((2, 5, PLANES)),
         dma((2, 4)),
         dma((2, 4)),
-        dma((3, max(group, ny))),
-        dma((3, max(group, ny))),
+        dma((5, max(nx, ny))),
+        dma((5, max(nx, ny))),
+        dma((10,)),
     ]
 
-    def on_device(*operands):
+    shapes = (
+        block,
+        block,
+        jax.ShapeDtypeStruct((40, HID), f32),
+        jax.ShapeDtypeStruct((HID, HID), f32),
+        jax.ShapeDtypeStruct((HID, HID), f32),
+        jax.ShapeDtypeStruct((FIELDS, HID), f32),
+        jax.ShapeDtypeStruct((3, HID), f32),
+        jax.ShapeDtypeStruct((1, FIELDS), f32),
+    )
+    anywhere = pl.BlockSpec(memory_space=pl.ANY)
+
+    def on_device(state, cotangent, diffusion, w_in, w_second, w_third, w_out, biases, bias_out):
         outs = pl.pallas_call(
             functools.partial(kernel, sizes, scale),
-            out_shape=(
-                block,
-                block,
-                jax.ShapeDtypeStruct((40, HID), f32),
-                jax.ShapeDtypeStruct((HID, HID), f32),
-                jax.ShapeDtypeStruct((HID, HID), f32),
-                jax.ShapeDtypeStruct((HID, FIELDS), f32),
-                jax.ShapeDtypeStruct((3, HID), f32),
-                jax.ShapeDtypeStruct((1, FIELDS), f32),
-            ),
-            in_specs=[vmem] * 8 + [pl.BlockSpec(memory_space=pltpu.SMEM)],
-            out_specs=[vmem] * 8,
+            out_shape=shapes,
+            in_specs=[anywhere] * 8 + [pl.BlockSpec(memory_space=pltpu.SMEM)],
+            out_specs=[anywhere] * 2 + [vmem] * 6,
             scratch_shapes=scratch,
             compiler_params=pltpu.CompilerParams(
                 collective_id=0, has_side_effects=True, vmem_limit_bytes=60 * 2**20
             ),
             name="two_steps_and_adjoint",
-        )(*operands)
-        return outs[:7] + (outs[7].reshape(FIELDS),)
+        )(state, cotangent, diffusion, w_in, w_second, w_third, w_out.T, biases, bias_out)
+        outs = pl.pallas_call(
+            deliver,
+            out_shape=shapes,
+            in_specs=[anywhere] * 8,
+            out_specs=[anywhere] * 8,
+            scratch_shapes=[dma((8,))],
+            compiler_params=pltpu.CompilerParams(vmem_limit_bytes=60 * 2**20),
+            name="deliver",
+        )(*outs)
+        return outs[:5] + (outs[5].T, outs[6], outs[7].reshape(FIELDS))
 
     fields = P(None, "gz", "gy", "gx")
     placed = (fields, fields, P("gz", "gy", "gx")) + (P(),) * 6

time: 88.3 us -> 86.3 us (0.977)
  local copies, waits for them, and re-layouts: 8.6 us -> 0 us
  Pallas kernels: 78.7 us -> 85.5 us
    unnamed x21 -> x0, local copies, waits for them, and re-layouts: 8.6 us -> none
    pallas_call x1 -> x2, Pallas kernels: 78.7 us -> 85.5 us  [the longest x1 67.7 us: on_device(): pl.pallas_call(functools.partial(kernel, sizes, scale), out_shape=shapes,...]
where the time goes in v2:
time: 86.3 us; the launch traced here: 86.2 us
  Pallas kernels  85.5 us (99%)
    pallas_call x1, Pallas kernels, on_device(): pl.pallas_call(functools.partial(kernel, sizes, scale), out_shape=shapes,...  67.7 us
    pallas_call x1, Pallas kernels, on_device(): pl.pallas_call(deliver, out_shape=shapes, in_specs=[anywhere] * 8, out_sp...  17.8 us

profile of v2, /device:TPU:1, one launch (start us, length us, event | category | flops | bytes accessed | tf_op | source)
XLA Modules:
  0.0 86.2 jit_solution(12193469364081160642)
XLA Ops:
  0.6 67.7 %two_steps_and_adjoint.1 = (f32[4,6,16,128]{3,2,1,0:T(8,128)}, f32[4,6,16,128]{3,2,1,0:T(8,128)}, f32[40,128]{1,0:T(8,128)}, f32[128,128]{1,0:T(8,128)}, f32[128...) custom-call(f32[4,6,16,128]{3,2,1,0:T(8,128)} %state_in.1, f32[4,6,16,128]{3,2,1,0:T(8,128)} %cot_in.1, ...), custom_call_target="tpu_custom_call" | custom-call | tf_op jit(solution)/shard_map/two_steps_and_adjoint/pallas_call | solution.py:921
  68.4 17.8 %deliver.1 = (f32[4,6,16,128]{3,2,1,0:T(8,128)}, f32[4,6,16,128]{3,2,1,0:T(8,128)}, f32[40,128]{1,0:T(8,128)}, f32[128,128]{1,0:T(8,128)}, f32[128,128]{1,0:T(8,...) custom-call(f32[4,6,16,128]{3,2,1,0:T(8,128)} %get-tuple-element.24.refs_0_, ...), custom_call_target="tpu_custom_call" | custom-call | tf_op jit(solution)/shard_map/deliver/pallas_call | solution.py:932

commit v3 on v2

--- a/solution.py
+++ b/solution.py
@@ -100,12 +100,7 @@
     bias_out,
     final_out,
     adjoint_out,
-    g_in_out,
-    g_second_out,
-    g_third_out,
-    g_readout_out,
-    g_biases_out,
-    g_bias_out_out,
+    sums_out,
     state_here,
     cot_here,
     diff_here,
@@ -154,6 +149,7 @@
     g_two,
     g_three,
     g_four,
+    g_last,
     sums,
     landed_pair,
     landed_a,
@@ -292,11 +288,13 @@
         for each in copies:
             each.wait_send()
 
-    def send_fields(e, z):
+    def pack_fields(e, z):
         plane = st[e, z + 1]
         empty = jnp.zeros((8, LANES), f32)
         p_first[e, z] = pack_lane(plane, 0, 0, empty)
         p_last[e, z] = pack_lane(plane, LANES - 1, 0, empty)
+
+    def send_fields(e, z):
         start(field_copies(e, z))
 
         @pl.when(z == 0)
@@ -315,6 +313,7 @@
     def lay_out(z, carry):
         for k in range(FIELDS):
             st[0, z + 1, pl.ds(k, 16, stride=FIELDS), :] = state_here[k, z]
+        pack_fields(0, z)
         return carry
 
     fetches[0].wait()
@@ -391,7 +390,7 @@
     for k in range(FIELDS):
         bias_tile = jnp.where(field_row == k, bias_out[k], bias_tile)
     bias_plane = jnp.concatenate([bias_tile] * 8, axis=0)
-    for each in (g_one, g_two, g_three, g_four):
+    for each in (g_one, g_two, g_three, g_four, g_last):
         each[...] = jnp.zeros(each.shape, f32)
 
     lane = lane_index(ROWS)
@@ -459,17 +458,18 @@
 
     def grad_rows(adjoint):
         scaled = wide_of(time_step * adjoint)
-        return jnp.concatenate([scaled, jnp.zeros((8, WIDE), f32)], axis=0).astype(bf16)
+        rounded = jnp.concatenate([scaled, jnp.zeros((8, WIDE), f32)], axis=0).astype(bf16)
+        added = rounded.astype(f32)[0:8]
+        for part in range(8):
+            g_last[...] += added[:, LANES * part : LANES * (part + 1)]
+        return rounded
 
     def backward(features, values, doubled, grad_out):
-        ones_here = ones_cells[:, :sub_width]
         back_three = times(side_by_side(mm(v_out[...], grad_out)), doubled[2])
         yield
         back_two = times(mm(v_three[...], back_three), doubled[1])
         yield
-        g_four[:, 0:16] += mm_cells(
-            jnp.concatenate([stacked_of(values[2]), ones_here], axis=0), grad_out
-        )
+        g_four[...] += mm_cells(grad_out, stacked_of(values[2]))
         back_one = stacked_of(times(mm(v_two[...], back_two), doubled[0]))
         yield
         g_three[...] += mm_cells(jnp.concatenate([values[1], ones_cells], axis=0), back_three)
@@ -619,6 +619,7 @@
 
         outs = in_turn([forward(sub) for sub in range(SUBS)])
         st[1, z + 1] = stepped(points, z, jnp.concatenate(outs, axis=1))
+        pack_fields(1, z)
         send_fields(1, z)
         return carry
 
@@ -671,17 +672,19 @@
     one = g_one[...]
     merged = one[:, :HID] + jnp.concatenate([one[4:, HID:], one[:4, HID:]], axis=0)
     first_rows = jnp.concatenate([merged[8 * j : 8 * j + 4] for j in range(STENCIL)], axis=0)
-    four = g_four[...]
-    shifted = four[:HID] + pltpu.roll(four[HID : 2 * HID], LANES - FIELDS, 1)
-    last = four[2 * HID : 2 * HID + 8]
-    last = last + pltpu.roll(last, LANES - FIELDS, 1)
+    readout_rows = g_four[0:4, :HID] + g_four[4:8, HID:]
+    last = jnp.sum(g_last[...], axis=1, keepdims=True)
+    last = last[0:4] + last[4:8]
+    row = lax.broadcasted_iota(jnp.int32, (FIELDS, LANES), 0)
+    column = lax.broadcasted_iota(jnp.int32, (FIELDS, LANES), 1)
+    last = jnp.sum(jnp.where(row == column, last, 0.0), axis=0, keepdims=True)
     rest = jnp.concatenate(
         [
             one[80:81, :HID] + one[80:81, HID:],
             g_two[HID : HID + 1],
             g_three[HID : HID + 1],
-            last[0:1],
-            shifted.T[0:4],
+            last,
+            readout_rows,
         ],
         axis=0,
     )
@@ -797,28 +800,64 @@
     each(1, nx, pass_on)
     each(0, nx, lambda step: hand_over_in(step).wait_recv())
 
-    whole = total[...].reshape(SUMS, LANES)
-    g_second_out[...] = whole[0:HID]
-    g_third_out[...] = whole[HID : 2 * HID]
-    g_in_out[...] = whole[2 * HID : 2 * HID + 40]
-    tail = whole[296:304]
+    sums_copy = pltpu.make_async_copy(total, sums_out, here_sem.at[10])
+    sums_copy.start()
+    each(1, nx, lambda step: spread_out(step).wait_send())
+    each(0, nx, lambda step: hand_over(step).wait_send())
+    sums_copy.wait()
+
+
+def deliver(
+    final_in,
+    adjoint_in,
+    sums_in,
+    final_out,
+    adjoint_out,
+    g_in_out,
+    g_second_out,
+    g_third_out,
+    g_readout_out,
+    g_biases_out,
+    g_bias_out_out,
+    final_here,
+    adjoint_here,
+    sums_here,
+    load_sem,
+    store_sem,
+):
+    loads = [
+        pltpu.make_async_copy(source, target, load_sem.at[number])
+        for number, (source, target) in enumerate(
+            ((sums_in, sums_here), (final_in, final_here), (adjoint_in, adjoint_here))
+        )
+    ]
+    stores = [
+        pltpu.make_async_copy(source, target, store_sem.at[number])
+        for number, (source, target) in enumerate(
+            (
+                (final_here, final_out),
+                (adjoint_here, adjoint_out),
+                (sums_here.at[pl.ds(0, HID)], g_second_out),
+                (sums_here.at[pl.ds(HID, HID)], g_third_out),
+                (sums_here.at[pl.ds(2 * HID, 40)], g_in_out),
+            )
+        )
+    ]
+    for load in loads:
+        load.start()
+    loads[1].wait()
+    stores[0].start()
+    loads[2].wait()
+    stores[1].start()
+    loads[0].wait()
+    for store in stores[2:]:
+        store.start()
+    tail = sums_here[296:304]
     g_biases_out[...] = tail[0:3]
     g_readout_out[...] = tail[4:8]
     g_bias_out_out[...] = tail[3:4, 0:FIELDS]
-    each(1, nx, lambda step: spread_out(step).wait_send())
-    each(0, nx, lambda step: hand_over(step).wait_send())
-
-
-def deliver(*refs):
-    count = (len(refs) - 1) // 2
-    copies = [
-        pltpu.make_async_copy(refs[number], refs[count + number], refs[-1].at[number])
-        for number in range(count)
-    ]
-    for each in copies:
-        each.start()
-    for each in copies:
-        each.wait()
+    for store in stores:
+        store.wait()
 
 
 def solution(mesh):
@@ -886,7 +925,8 @@
         buffer(96, 2 * HID),
         buffer(144, HID),
         buffer(144, HID),
-        buffer(2 * HID + 16, LANES),
+        buffer(16, 2 * HID),
+        buffer(8, LANES),
         buffer(nz, nx, share, LANES),
         buffer(nx, share, LANES),
         buffer(nx, share, LANES),
@@ -902,7 +942,7 @@
         dma((2, 4)),
         dma((5, max(nx, ny))),
         dma((5, max(nx, ny))),
-        dma((10,)),
+        dma((11,)),
     ]
 
     shapes = (
@@ -920,9 +960,9 @@
     def on_device(state, cotangent, diffusion, w_in, w_second, w_third, w_out, biases, bias_out):
         outs = pl.pallas_call(
             functools.partial(kernel, sizes, scale),
-            out_shape=shapes,
+            out_shape=(block, block, jax.ShapeDtypeStruct((nz, nx, share, LANES), f32)),
             in_specs=[anywhere] * 8 + [pl.BlockSpec(memory_space=pltpu.SMEM)],
-            out_specs=[anywhere] * 2 + [vmem] * 6,
+            out_specs=[anywhere] * 3,
             scratch_shapes=scratch,
             compiler_params=pltpu.CompilerParams(
                 collective_id=0, has_side_effects=True, vmem_limit_bytes=60 * 2**20
@@ -932,12 +972,18 @@
         outs = pl.pallas_call(
             deliver,
             out_shape=shapes,
-            in_specs=[anywhere] * 8,
-            out_specs=[anywhere] * 8,
-            scratch_shapes=[dma((8,))],
+            in_specs=[anywhere] * 3,
+            out_specs=[anywhere] * 5 + [vmem] * 3,
+            scratch_shapes=[
+                buffer(FIELDS, PLANES, 16, LANES),
+                buffer(FIELDS, PLANES, 16, LANES),
+                buffer(SUMS, LANES),
+                dma((3,)),
+                dma((5,)),
+            ],
             compiler_params=pltpu.CompilerParams(vmem_limit_bytes=60 * 2**20),
             name="deliver",
-        )(*outs)
+        )(outs[0], outs[1], outs[2].reshape(SUMS, LANES))
         return outs[:5] + (outs[5].T, outs[6], outs[7].reshape(FIELDS))
 
     fields = P(None, "gz", "gy", "gx")

time: 86.3 us -> 70.7 us (0.82)
  Pallas kernels: 85.5 us -> 69.9 us
    pallas_call x2, Pallas kernels: 85.5 us -> 69.9 us  [the longest x1 67.5 us: on_device(): pl.pallas_call(functools.partial(kernel, sizes, scale), out_shape=(block,...]
where the time goes in v3:
time: 70.7 us; the launch traced here: 70.6 us
  Pallas kernels  69.9 us (99%)
    pallas_call x1, Pallas kernels, on_device(): pl.pallas_call(functools.partial(kernel, sizes, scale), out_shape=(block,...  67.5 us
    pallas_call x1, Pallas kernels, on_device(): pl.pallas_call(deliver, out_shape=shapes, in_specs=[anywhere] * 3, out_sp...  2.49 us

profile of v3, /device:TPU:1, one launch (start us, length us, event | category | flops | bytes accessed | tf_op | source)
XLA Modules:
  0.0 70.6 jit_solution(12827665526773490133)
XLA Ops:
  0.6 67.5 %two_steps_and_adjoint.1 = (f32[4,6,16,128]{3,2,1,0:T(8,128)}, f32[4,6,16,128]{3,2,1,0:T(8,128)}, f32[2,8,24,128]{3,2,1,0:T(8,128)}) custom-call(f32[4,6,16,128]{3,2,1,0:T(8,128)} %state_in.1, f32[4,6,16,128]{3,2,1,0:T(8,128)} %cot_in.1, f32[6,16,128]{2,1,0:T(8,128)} %diff_in.1, bf16[40,128]{1,0:T(8,128)(2,1)} %w_in.1, bf16[128,128]{1,0:T(8,128)(2,1)} %w_second.1, ...), custom_call_target="tpu_custom_call" | custom-call | tf_op jit(solution)/shard_map/two_steps_and_adjoint/pallas_call | solution.py:961
  68.1 2.5 %deliver.1 = (f32[4,6,16,128]{3,2,1,0:T(8,128)}, f32[4,6,16,128]{3,2,1,0:T(8,128)}, f32[40,128]{1,0:T(8,128)}, f32[128,128]{1,0:T(8,128)}, f32[128,128]{1,0:T(8,...) custom-call(f32[4,6,16,128]{3,2,1,0:T(8,128)} %get-tuple-element.19.final_in, ...), custom_call_target="tpu_custom_call" | custom-call | tf_op jit(solution)/shard_map/deliver/pallas_call | solution.py:972

commit v4 on v3

--- a/solution.py
+++ b/solution.py
@@ -109,8 +109,6 @@
     w_third_here,
     w_out_here,
     biases_here,
-    final_here,
-    adjoint_here,
     st,
     p_first,
     p_last,
@@ -310,6 +308,12 @@
         half = lax.div(step, 2)
         return half + odd * (PLANES - 1 - 2 * half)
 
+    def first_place(step):
+        after = lax.max(step - 1, 0)
+        odd = lax.rem(after, 2)
+        half = lax.div(after, 2)
+        return lax.min(step, 1) * (1 + half + odd * (PLANES - 2 - 2 * half))
+
     def lay_out(z, carry):
         for k in range(FIELDS):
             st[0, z + 1, pl.ds(k, 16, stride=FIELDS), :] = state_here[k, z]
@@ -321,7 +325,7 @@
     pl.semaphore_wait(barrier, 7 + (nx - 1) + (ny - 1))
 
     def first_sends(step, carry):
-        send_fields(0, place(step))
+        send_fields(0, first_place(step))
         return carry
 
     lax.fori_loop(0, PLANES, first_sends, 0)
@@ -464,20 +468,25 @@
             g_last[...] += added[:, LANES * part : LANES * (part + 1)]
         return rounded
 
-    def backward(features, values, doubled, grad_out):
+    def chain(values, doubled, grad_out):
         back_three = times(side_by_side(mm(v_out[...], grad_out)), doubled[2])
         yield
         back_two = times(mm(v_three[...], back_three), doubled[1])
         yield
-        g_four[...] += mm_cells(grad_out, stacked_of(values[2]))
         back_one = stacked_of(times(mm(v_two[...], back_two), doubled[0]))
         yield
-        g_three[...] += mm_cells(jnp.concatenate([values[1], ones_cells], axis=0), back_three)
-        yield
-        g_two[...] += mm_cells(jnp.concatenate([values[0], ones_cells], axis=0), back_two)
-        yield
-        g_one[...] += mm_cells(features, back_one)
-        return back_one
+        return back_three, back_two, back_one
+
+    def add_terms(features, values, grad_out, backs_of, order):
+        for layer in order:
+            if layer == 4:
+                g_four[...] += mm_cells(grad_out, stacked_of(values[2]))
+            elif layer == 1:
+                g_one[...] += mm_cells(features, backs_of[2])
+            else:
+                total_of = g_three if layer == 3 else g_two
+                cells = jnp.concatenate([values[layer - 2], ones_cells], axis=0)
+                total_of[...] += mm_cells(cells, backs_of[3 - layer])
 
     def in_turn(pieces):
         results = [None] * len(pieces)
@@ -539,6 +548,30 @@
         result = result + rows_up(q[e, here, 3] + q[e, z, 8], rows_in[4:8])
         return result + rows_down(q[e, here, 4], yb[e, z][0:4])
 
+    def await_first(step):
+        @pl.when(step == 0)
+        def _():
+            arrive(field_copies(0, 0))
+            arrive(field_copies(0, 1))
+            arrive(field_copies_high(0))
+
+        @pl.when(step == 1)
+        def _():
+            arrive(field_copies(0, 2))
+
+        @pl.when(step == 2)
+        def _():
+            arrive(field_copies(0, 5))
+            arrive(field_copies_low(0))
+
+        @pl.when(step == 3)
+        def _():
+            arrive(field_copies(0, 3))
+
+        @pl.when(step == 4)
+        def _():
+            arrive(field_copies(0, 4))
+
     def await_fields(e, step):
         @pl.when(step == 0)
         def _():
@@ -603,8 +636,8 @@
             target[k, z] = staged[pl.ds(k, 16, stride=FIELDS), :]
 
     def first_step(step, carry):
-        z = place(step)
-        await_fields(0, step)
+        z = first_place(step)
+        await_first(step)
         points = stencil(0, z)
         features = arrange(points)
         feats[z] = features
@@ -633,23 +666,27 @@
         adjoint = cot[z]
         grad_out = grad_rows(adjoint)
 
-        def both_ways(sub):
+        def forward(sub):
             values, doubled = [], []
             yield from layers(features[:, piece(sub)], values, doubled)
-            out = readout_of(values[2])
-            back_one = yield from backward(
-                features[:, piece(sub)], values, doubled, grad_out[:, piece(sub)]
+            return values, doubled, readout_of(values[2])
+
+        passed = in_turn([forward(sub) for sub in range(SUBS)])
+        put(final_out, z, stepped(points, z, jnp.concatenate([one[2] for one in passed], axis=1)))
+        chains = in_turn([chain(*passed[sub][0:2], grad_out[:, piece(sub)]) for sub in range(SUBS)])
+        wides = [mm(v_one[...], backs_of[2]) for backs_of in chains]
+        send_adjoint(0, z, jnp.concatenate(wides, axis=1), adjoint)
+        for sub in range(SUBS):
+            add_terms(
+                features[:, piece(sub)],
+                passed[sub][0],
+                grad_out[:, piece(sub)],
+                chains[sub],
+                (4, 3, 2, 1),
             )
-            return out, mm(v_one[...], back_one)
-
-        outs, wides = zip(*in_turn([both_ways(sub) for sub in range(SUBS)]))
-        put(final_here, z, stepped(points, z, jnp.concatenate(outs, axis=1)))
-        send_adjoint(0, z, jnp.concatenate(wides, axis=1), adjoint)
         return carry
 
     lax.fori_loop(0, PLANES, second_step, 0)
-    final_copy = pltpu.make_async_copy(final_here, final_out, here_sem.at[8])
-    final_copy.start()
 
     def first_back(step, carry):
         z = place(step)
@@ -658,13 +695,22 @@
         adj_mid[z] = adjoint
         grad_out = grad_rows(adjoint)
 
-        def back(sub):
-            values = [acts[layer, z, :, beside(sub)] for layer in range(3)]
-            doubled = [slopes[layer, z, :, beside(sub)] for layer in range(3)]
-            return backward(feats[z, :, piece(sub)], values, doubled, grad_out[:, piece(sub)])
-
-        for sub, back_one in enumerate(in_turn([back(sub) for sub in range(SUBS)])):
-            backs[z, :, piece(sub)] = back_one
+        values, doubled = [
+            [[kept[layer, z, :, beside(sub)] for layer in range(3)] for sub in range(SUBS)]
+            for kept in (acts, slopes)
+        ]
+        chains = in_turn(
+            [chain(values[sub], doubled[sub], grad_out[:, piece(sub)]) for sub in range(SUBS)]
+        )
+        for sub in range(SUBS):
+            backs[z, :, piece(sub)] = chains[sub][2]
+            add_terms(
+                feats[z, :, piece(sub)],
+                values[sub],
+                grad_out[:, piece(sub)],
+                chains[sub],
+                (1, 2, 3, 4),
+            )
         return carry
 
     lax.fori_loop(0, PLANES, first_back, 0)
@@ -747,7 +793,7 @@
     def last_gather(step, carry):
         z = place(step)
         await_adjoint(1, step)
-        put(adjoint_here, z, gather(1, z, adj_mid[z]))
+        put(adjoint_out, z, gather(1, z, adj_mid[z]))
         return carry
 
     pair.start()
@@ -764,8 +810,6 @@
     each(1, ny, lambda step: across(step).start())
 
     lax.fori_loop(0, PLANES, last_gather, 0)
-    adjoint_copy = pltpu.make_async_copy(adjoint_here, adjoint_out, here_sem.at[9])
-    adjoint_copy.start()
 
     each(1, ny, lambda step: across_in(step).wait_recv())
     held = landed_b[0]
@@ -790,8 +834,6 @@
     pair.wait_send()
     each(1, nx, lambda step: scatter(step).wait_send())
     each(1, ny, lambda step: across(step).wait_send())
-    final_copy.wait()
-    adjoint_copy.wait()
 
     def pass_on(step):
         spread_in(step).wait_recv()
@@ -800,11 +842,9 @@
     each(1, nx, pass_on)
     each(0, nx, lambda step: hand_over_in(step).wait_recv())
 
-    sums_copy = pltpu.make_async_copy(total, sums_out, here_sem.at[10])
-    sums_copy.start()
+    sums_out[...] = total[...].reshape(SUMS, LANES)
     each(1, nx, lambda step: spread_out(step).wait_send())
     each(0, nx, lambda step: hand_over(step).wait_send())
-    sums_copy.wait()
 
 
 def deliver(
@@ -819,40 +859,23 @@
     g_readout_out,
     g_biases_out,
     g_bias_out_out,
-    final_here,
-    adjoint_here,
-    sums_here,
-    load_sem,
     store_sem,
 ):
-    loads = [
-        pltpu.make_async_copy(source, target, load_sem.at[number])
-        for number, (source, target) in enumerate(
-            ((sums_in, sums_here), (final_in, final_here), (adjoint_in, adjoint_here))
-        )
-    ]
     stores = [
         pltpu.make_async_copy(source, target, store_sem.at[number])
         for number, (source, target) in enumerate(
             (
-                (final_here, final_out),
-                (adjoint_here, adjoint_out),
-                (sums_here.at[pl.ds(0, HID)], g_second_out),
-                (sums_here.at[pl.ds(HID, HID)], g_third_out),
-                (sums_here.at[pl.ds(2 * HID, 40)], g_in_out),
+                (final_in, final_out),
+                (adjoint_in, adjoint_out),
+                (sums_in.at[pl.ds(0, HID)], g_second_out),
+                (sums_in.at[pl.ds(HID, HID)], g_third_out),
+                (sums_in.at[pl.ds(2 * HID, 40)], g_in_out),
             )
         )
     ]
-    for load in loads:
-        load.start()
-    loads[1].wait()
-    stores[0].start()
-    loads[2].wait()
-    stores[1].start()
-    loads[0].wait()
-    for store in stores[2:]:
+    for store in stores:
         store.start()
-    tail = sums_here[296:304]
+    tail = sums_in[296:304]
     g_biases_out[...] = tail[0:3]
     g_readout_out[...] = tail[4:8]
     g_bias_out_out[...] = tail[3:4, 0:FIELDS]
@@ -886,8 +909,6 @@
         packed(HID, HID),
         packed(FIELDS, HID),
         buffer(3, HID),
-        buffer(FIELDS, PLANES, 16, LANES),
-        buffer(FIELDS, PLANES, 16, LANES),
         buffer(2, PLANES + 2, ROWS, LANES),
         buffer(2, PLANES, *tile),
         buffer(2, PLANES, *tile),
@@ -960,30 +981,28 @@
     def on_device(state, cotangent, diffusion, w_in, w_second, w_third, w_out, biases, bias_out):
         outs = pl.pallas_call(
             functools.partial(kernel, sizes, scale),
-            out_shape=(block, block, jax.ShapeDtypeStruct((nz, nx, share, LANES), f32)),
-            in_specs=[anywhere] * 8 + [pl.BlockSpec(memory_space=pltpu.SMEM)],
-            out_specs=[anywhere] * 3,
+            out_shape=(
+                buffer(FIELDS, PLANES, 16, LANES),
+                buffer(FIELDS, PLANES, 16, LANES),
+                buffer(SUMS, LANES),
+            ),
+            in_specs=[pl.BlockSpec(memory_space=pl.ANY)] * 8 + [pl.BlockSpec(memory_space=pltpu.SMEM)],
+            out_specs=[vmem] * 3,
             scratch_shapes=scratch,
             compiler_params=pltpu.CompilerParams(
-                collective_id=0, has_side_effects=True, vmem_limit_bytes=60 * 2**20
+                collective_id=0, has_side_effects=True, vmem_limit_bytes=58 * 2**20
             ),
             name="two_steps_and_adjoint",
         )(state, cotangent, diffusion, w_in, w_second, w_third, w_out.T, biases, bias_out)
         outs = pl.pallas_call(
             deliver,
             out_shape=shapes,
-            in_specs=[anywhere] * 3,
+            in_specs=[vmem] * 3,
             out_specs=[anywhere] * 5 + [vmem] * 3,
-            scratch_shapes=[
-                buffer(FIELDS, PLANES, 16, LANES),
-                buffer(FIELDS, PLANES, 16, LANES),
-                buffer(SUMS, LANES),
-                dma((3,)),
-                dma((5,)),
-            ],
-            compiler_params=pltpu.CompilerParams(vmem_limit_bytes=60 * 2**20),
+            scratch_shapes=[dma((5,))],
+            compiler_params=pltpu.CompilerParams(vmem_limit_bytes=16 * 2**20),
             name="deliver",
-        )(outs[0], outs[1], outs[2].reshape(SUMS, LANES))
+        )(*outs)
         return outs[:5] + (outs[5].T, outs[6], outs[7].reshape(FIELDS))
 
     fields = P(None, "gz", "gy", "gx")

time: 70.7 us -> 69.9 us (0.989)
    pallas_call x2, Pallas kernels: 69.9 us -> 69.2 us  [the longest x1 67.8 us: on_device(): pl.pallas_call(functools.partial(kernel, sizes, scale), out_shape=(buffer...]
where the time goes in v4:
time: 69.9 us; the launch traced here: 69.8 us
  Pallas kernels  69.2 us (99%)
    pallas_call x1, Pallas kernels, on_device(): pl.pallas_call(functools.partial(kernel, sizes, scale), out_shape=(buffer...  67.8 us
    pallas_call x1, Pallas kernels, on_device(): pl.pallas_call(deliver, out_shape=shapes, in_specs=[vmem] * 3, out_specs=...  1.41 us

profile of v4, /device:TPU:1, one launch (start us, length us, event | category | flops | bytes accessed | tf_op | source)
XLA Modules:
  0.0 69.8 jit_solution(6001964805024479207)
XLA Ops:
  0.6 67.8 %two_steps_and_adjoint.1 = (f32[4,6,16,128]{3,2,1,0:T(8,128)S(1)}, f32[4,6,16,128]{3,2,1,0:T(8,128)S(1)}, f32[384,128]{1,0:T(8,128)S(1)}) custom-call(f32[4,6,16,128]{3,2,1,0:T(8,128)} %state_in.1, f32[4,6,16,128]{3,2,1,0:T(8,128)} %cot_in.1, f32[6,16,128]{2,1,0:T(8,128)} %diff_in.1, bf16[40,128]{1,0:T(8,128)(2,1)} %w_in.1, bf16[128,128]{1,0:T(8,128)(2,1)} %w_second.1, ...), custom_call_target="tpu_custom_call" | custom-call | tf_op jit(solution)/shard_map/two_steps_and_adjoint/pallas_call | solution.py:982
  68.4 1.4 %deliver.1 = (f32[4,6,16,128]{3,2,1,0:T(8,128)}, f32[4,6,16,128]{3,2,1,0:T(8,128)}, f32[40,128]{1,0:T(8,128)}, f32[128,128]{1,0:T(8,128)}, f32[128,128]{1,0:T(8,...) custom-call(f32[4,6,16,128]{3,2,1,0:T(8,128)S(1)} %get-tuple-element.19.final_in, ...), custom_call_target="tpu_custom_call" | custom-call | tf_op jit(solution)/shard_map/deliver/pallas_call | solution.py:997

commit v5 on v4

--- a/solution.py
+++ b/solution.py
@@ -21,7 +21,7 @@
 WIDE = 1024
 HID = 128
 SUMS = 384
-SUBS = 2
+SUBS = 4
 
 
 def mm(former, latter):
@@ -468,25 +468,21 @@
             g_last[...] += added[:, LANES * part : LANES * (part + 1)]
         return rounded
 
-    def chain(values, doubled, grad_out):
+    def backward(features, values, doubled, grad_out, to_features):
         back_three = times(side_by_side(mm(v_out[...], grad_out)), doubled[2])
         yield
         back_two = times(mm(v_three[...], back_three), doubled[1])
         yield
+        g_four[...] += mm_cells(grad_out, stacked_of(values[2]))
         back_one = stacked_of(times(mm(v_two[...], back_two), doubled[0]))
         yield
-        return back_three, back_two, back_one
-
-    def add_terms(features, values, grad_out, backs_of, order):
-        for layer in order:
-            if layer == 4:
-                g_four[...] += mm_cells(grad_out, stacked_of(values[2]))
-            elif layer == 1:
-                g_one[...] += mm_cells(features, backs_of[2])
-            else:
-                total_of = g_three if layer == 3 else g_two
-                cells = jnp.concatenate([values[layer - 2], ones_cells], axis=0)
-                total_of[...] += mm_cells(cells, backs_of[3 - layer])
+        g_three[...] += mm_cells(jnp.concatenate([values[1], ones_cells], axis=0), back_three)
+        result = mm(v_one[...], back_one) if to_features else back_one
+        yield
+        g_two[...] += mm_cells(jnp.concatenate([values[0], ones_cells], axis=0), back_two)
+        yield
+        g_one[...] += mm_cells(features, back_one)
+        return result
 
     def in_turn(pieces):
         results = [None] * len(pieces)
@@ -604,21 +600,21 @@
 
         @pl.when(step == 1)
         def _():
+            arrive(adjoint_copies(e, 1))
+
+        @pl.when(step == 2)
+        def _():
             arrive(adjoint_copies(e, 5))
             arrive(adjoint_copies(e, 4))
             arrive(adjoint_copies_low(e))
 
-        @pl.when(step == 2)
-        def _():
-            arrive(adjoint_copies(e, 1))
-
         @pl.when(step == 3)
         def _():
+            arrive(adjoint_copies(e, 2))
+
+        @pl.when(step == 4)
+        def _():
             arrive(adjoint_copies(e, 3))
-
-        @pl.when(step == 4)
-        def _():
-            arrive(adjoint_copies(e, 2))
 
     def piece(sub):
         return slice(sub * sub_width, (sub + 1) * sub_width)
@@ -673,44 +669,33 @@
 
         passed = in_turn([forward(sub) for sub in range(SUBS)])
         put(final_out, z, stepped(points, z, jnp.concatenate([one[2] for one in passed], axis=1)))
-        chains = in_turn([chain(*passed[sub][0:2], grad_out[:, piece(sub)]) for sub in range(SUBS)])
-        wides = [mm(v_one[...], backs_of[2]) for backs_of in chains]
+        wides = in_turn(
+            [
+                backward(features[:, piece(sub)], *passed[sub][0:2], grad_out[:, piece(sub)], True)
+                for sub in range(SUBS)
+            ]
+        )
         send_adjoint(0, z, jnp.concatenate(wides, axis=1), adjoint)
-        for sub in range(SUBS):
-            add_terms(
-                features[:, piece(sub)],
-                passed[sub][0],
-                grad_out[:, piece(sub)],
-                chains[sub],
-                (4, 3, 2, 1),
-            )
         return carry
 
     lax.fori_loop(0, PLANES, second_step, 0)
 
     def first_back(step, carry):
-        z = place(step)
+        z = first_place(step)
         await_adjoint(0, step)
         adjoint = gather(0, z, cot[z])
         adj_mid[z] = adjoint
         grad_out = grad_rows(adjoint)
 
-        values, doubled = [
-            [[kept[layer, z, :, beside(sub)] for layer in range(3)] for sub in range(SUBS)]
-            for kept in (acts, slopes)
-        ]
-        chains = in_turn(
-            [chain(values[sub], doubled[sub], grad_out[:, piece(sub)]) for sub in range(SUBS)]
-        )
-        for sub in range(SUBS):
-            backs[z, :, piece(sub)] = chains[sub][2]
-            add_terms(
-                feats[z, :, piece(sub)],
-                values[sub],
-                grad_out[:, piece(sub)],
-                chains[sub],
-                (1, 2, 3, 4),
+        def back(sub):
+            values = [acts[layer, z, :, beside(sub)] for layer in range(3)]
+            doubled = [slopes[layer, z, :, beside(sub)] for layer in range(3)]
+            return backward(
+                feats[z, :, piece(sub)], values, doubled, grad_out[:, piece(sub)], False
             )
+
+        for sub, back_one in enumerate(in_turn([back(sub) for sub in range(SUBS)])):
+            backs[z, :, piece(sub)] = back_one
         return carry
 
     lax.fori_loop(0, PLANES, first_back, 0)
@@ -791,7 +776,7 @@
         return carry
 
     def last_gather(step, carry):
-        z = place(step)
+        z = first_place(step)
         await_adjoint(1, step)
         put(adjoint_out, z, gather(1, z, adj_mid[z]))
         return carry

time: 69.9 us -> 67.6 us (0.967)
  Pallas kernels: 69.2 us -> 66.8 us
    pallas_call x1, Pallas kernels: 67.8 us -> 65.4 us  [on_device(): pl.pallas_call(functools.partial(kernel, sizes, scale), out_shape=(buffer...]
where the time goes in v5:
time: 67.6 us; the launch traced here: 67.5 us
  Pallas kernels  66.8 us (99%)
    pallas_call x1, Pallas kernels, on_device(): pl.pallas_call(functools.partial(kernel, sizes, scale), out_shape=(buffer...  65.4 us
    pallas_call x1, Pallas kernels, on_device(): pl.pallas_call(deliver, out_shape=shapes, in_specs=[vmem] * 3, out_specs=...  1.41 us

profile of v5, /device:TPU:1, one launch (start us, length us, event | category | flops | bytes accessed | tf_op | source)
XLA Modules:
  0.0 67.5 jit_solution(15157237124858220251)
XLA Ops:
  0.6 65.4 %two_steps_and_adjoint.1 = (f32[4,6,16,128]{3,2,1,0:T(8,128)S(1)}, f32[4,6,16,128]{3,2,1,0:T(8,128)S(1)}, f32[384,128]{1,0:T(8,128)S(1)}) custom-call(f32[4,6,16,128]{3,2,1,0:T(8,128)} %state_in.1, f32[4,6,16,128]{3,2,1,0:T(8,128)} %cot_in.1, f32[6,16,128]{2,1,0:T(8,128)} %diff_in.1, bf16[40,128]{1,0:T(8,128)(2,1)} %w_in.1, bf16[128,128]{1,0:T(8,128)(2,1)} %w_second.1, ...), custom_call_target="tpu_custom_call" | custom-call | tf_op jit(solution)/shard_map/two_steps_and_adjoint/pallas_call | solution.py:967
  66.1 1.4 %deliver.1 = (f32[4,6,16,128]{3,2,1,0:T(8,128)}, f32[4,6,16,128]{3,2,1,0:T(8,128)}, f32[40,128]{1,0:T(8,128)}, f32[128,128]{1,0:T(8,128)}, f32[128,128]{1,0:T(8,...) custom-call(f32[4,6,16,128]{3,2,1,0:T(8,128)S(1)} %get-tuple-element.19.final_in, ...), custom_call_target="tpu_custom_call" | custom-call | tf_op jit(solution)/shard_map/deliver/pallas_call | solution.py:982

commit v6 on v5

--- a/solution.py
+++ b/solution.py
@@ -20,7 +20,8 @@
 LANES = 128
 WIDE = 1024
 HID = 128
-SUMS = 384
+FIRST_SUMS = 192
+SUMS = FIRST_SUMS + 128
 SUBS = 4
 
 
@@ -170,7 +171,8 @@
     right, left = lax.rem(gx + 1, nx), lax.rem(gx + nx - 1, nx)
     above, below = lax.rem(gy + 1, ny), lax.rem(gy + ny - 1, ny)
     other = 1 - gz
-    share = SUMS // nz // nx
+    share = FIRST_SUMS // nx
+    shares = (share, HID // nx)
 
     barrier = pltpu.get_barrier_semaphore()
 
@@ -178,8 +180,12 @@
         pl.semaphore_signal(barrier, inc=1, device_id=device, device_id_type=MESH)
 
     for device in (
+        (gx, above, gz),
+        (gx, below, gz),
         (right, above, gz),
         (left, below, gz),
+        (right, gy, gz),
+        (left, gy, gz),
         (gx, above, other),
         (gx, below, other),
         (right, gy, other),
@@ -192,13 +198,13 @@
         greet((lax.rem(gx + step, nx), gy, gz))
         return carry
 
-    lax.fori_loop(1, nx, greet_row, 0)
+    lax.fori_loop(2, max(nx - 1, 2), greet_row, 0)
 
     def greet_column(step, carry):
         greet((gx, lax.rem(gy + step, ny), gz))
         return carry
 
-    lax.fori_loop(1, ny, greet_column, 0)
+    lax.fori_loop(2, max(ny - 1, 2), greet_column, 0)
 
     fetches = [
         pltpu.make_async_copy(source, target, here_sem.at[number])
@@ -322,7 +328,7 @@
 
     fetches[0].wait()
     lax.fori_loop(0, PLANES, lay_out, 0)
-    pl.semaphore_wait(barrier, 7 + (nx - 1) + (ny - 1))
+    pl.semaphore_wait(barrier, 11 + max(nx - 3, 0) + max(ny - 3, 0))
 
     def first_sends(step, carry):
         send_fields(0, first_place(step))
@@ -720,40 +726,43 @@
         axis=0,
     )
     everything = jnp.concatenate(
-        [
-            g_two[0:HID],
-            g_three[0:HID],
-            first_rows,
-            rest,
-            jnp.zeros((SUMS - 304, LANES), f32),
-        ],
-        axis=0,
+        [g_two[0:HID], first_rows, rest, jnp.zeros((FIRST_SUMS - 176, LANES), f32)], axis=0
     )
-    sums[...] = everything.reshape(nz, nx, share, LANES)
+    sums[0] = everything.reshape(nx, share, LANES)
+    sums[1, :, 0 : shares[1]] = g_three[0:HID].reshape(nx, shares[1], LANES)
 
     pair = copy(sums.at[other], landed_pair, a_send.at[0, 0], a_recv.at[0, 0], (gx, gy, other))
 
-    def scatter(step):
+    def by_core(act):
+        for core in range(2):
+            pl.when(gz == core)(functools.partial(act, shares[core]))
+
+    def scatter(rows, step):
         target = lax.rem(gx + step, nx)
+        part = pl.ds(0, rows)
         return copy(
-            sums.at[gz, target], landed_a.at[step], a_send.at[1, step], a_recv.at[1, step], (target, gy, gz)
-        )
-
-    def across(step):
+            sums.at[gz, target, part], landed_a.at[step, part], a_send.at[1, step], a_recv.at[1, step], (target, gy, gz)
+        )
+
+    def across(rows, step):
         target = lax.rem(gy + step, ny)
-        return copy(landed_b.at[gy], landed_b.at[gy], a_send.at[2, step], a_recv.at[2, gy], (gx, target, gz))
-
-    def across_in(step):
+        part = pl.ds(0, rows)
+        return copy(landed_b.at[gy, part], landed_b.at[gy, part], a_send.at[2, step], a_recv.at[2, gy], (gx, target, gz))
+
+    def across_in(rows, step):
         source = lax.rem(gy + ny - step, ny)
-        return copy(landed_b.at[source], landed_b.at[source], a_send.at[2, step], a_recv.at[2, source], (gx, source, gz))
-
-    def spread_out(step):
+        part = pl.ds(0, rows)
+        return copy(landed_b.at[source, part], landed_b.at[source, part], a_send.at[2, step], a_recv.at[2, source], (gx, source, gz))
+
+    def spread_out(rows, step):
         target = lax.rem(gx + step, nx)
-        return copy(total.at[gz, gx], total.at[gz, gx], a_send.at[3, step], a_recv.at[3, gx], (target, gy, gz))
-
-    def spread_in(step):
+        part = pl.ds(0, rows)
+        return copy(total.at[gz, gx, part], total.at[gz, gx, part], a_send.at[3, step], a_recv.at[3, gx], (target, gy, gz))
+
+    def spread_in(rows, step):
         source = lax.rem(gx + nx - step, nx)
-        return copy(total.at[gz, source], total.at[gz, source], a_send.at[3, step], a_recv.at[3, source], (source, gy, gz))
+        part = pl.ds(0, rows)
+        return copy(total.at[gz, source, part], total.at[gz, source, part], a_send.at[3, step], a_recv.at[3, source], (source, gy, gz))
 
     def hand_over(step):
         source = lax.rem(gx + nx - step, nx)
@@ -769,6 +778,10 @@
             return carry
 
         lax.fori_loop(first, count, body, 0)
+
+    def near(turn):
+        half = lax.div(turn + 1, 2)
+        return half + (1 - lax.rem(turn, 2)) * (nx - 2 * half)
 
     def last_contributions(step, carry):
         z = place(step)
@@ -785,23 +798,23 @@
     lax.fori_loop(0, 2, last_contributions, 0)
     pair.wait_recv()
     sums[gz] = sums[gz] + landed_pair[...]
-    each(1, nx, lambda step: scatter(step).start())
+    by_core(lambda rows: each(1, nx, lambda turn: scatter(rows, near(nx - turn)).start()))
     lax.fori_loop(2, PLANES, last_contributions, 0)
-    each(1, nx, lambda step: scatter(step).wait_recv())
+    by_core(lambda rows: each(1, nx, lambda step: scatter(rows, step).wait_recv()))
     held = sums[gz, gx]
     for step in range(1, nx):
         held = held + landed_a[step]
     landed_b[gy] = held
-    each(1, ny, lambda step: across(step).start())
+    by_core(lambda rows: each(1, ny, lambda step: across(rows, step).start()))
 
     lax.fori_loop(0, PLANES, last_gather, 0)
 
-    each(1, ny, lambda step: across_in(step).wait_recv())
+    by_core(lambda rows: each(1, ny, lambda step: across_in(rows, step).wait_recv()))
     held = landed_b[0]
     for step in range(1, ny):
         held = held + landed_b[step]
     total[gz, gx] = held * scale
-    each(1, nx, lambda step: spread_out(step).start())
+    by_core(lambda rows: each(1, nx, lambda turn: spread_out(rows, near(nx - turn)).start()))
     hand_over(0).start()
 
     def finish_sends(z, carry):
@@ -817,18 +830,20 @@
         sent(adjoint_copies_low(e))
         sent(adjoint_copies_high(e))
     pair.wait_send()
-    each(1, nx, lambda step: scatter(step).wait_send())
-    each(1, ny, lambda step: across(step).wait_send())
-
-    def pass_on(step):
-        spread_in(step).wait_recv()
+    by_core(lambda rows: each(1, nx, lambda step: scatter(rows, step).wait_send()))
+    by_core(lambda rows: each(1, ny, lambda step: across(rows, step).wait_send()))
+
+    def pass_on(rows, turn):
+        step = near(turn)
+        spread_in(rows, step).wait_recv()
         hand_over(step).start()
 
-    each(1, nx, pass_on)
+    by_core(lambda rows: each(1, nx, functools.partial(pass_on, rows)))
     each(0, nx, lambda step: hand_over_in(step).wait_recv())
 
-    sums_out[...] = total[...].reshape(SUMS, LANES)
-    each(1, nx, lambda step: spread_out(step).wait_send())
+    sums_out[0:FIRST_SUMS] = total[0].reshape(FIRST_SUMS, LANES)
+    sums_out[FIRST_SUMS:SUMS] = total[1, :, 0 : shares[1]].reshape(HID, LANES)
+    by_core(lambda rows: each(1, nx, lambda step: spread_out(rows, step).wait_send()))
     each(0, nx, lambda step: hand_over(step).wait_send())
 
 
@@ -853,14 +868,14 @@
                 (final_in, final_out),
                 (adjoint_in, adjoint_out),
                 (sums_in.at[pl.ds(0, HID)], g_second_out),
-                (sums_in.at[pl.ds(HID, HID)], g_third_out),
-                (sums_in.at[pl.ds(2 * HID, 40)], g_in_out),
+                (sums_in.at[pl.ds(FIRST_SUMS, HID)], g_third_out),
+                (sums_in.at[pl.ds(HID, 40)], g_in_out),
             )
         )
     ]
     for store in stores:
         store.start()
-    tail = sums_in[296:304]
+    tail = sums_in[168:176]
     g_biases_out[...] = tail[0:3]
     g_readout_out[...] = tail[4:8]
     g_bias_out_out[...] = tail[3:4, 0:FIELDS]
@@ -871,7 +886,7 @@
 def solution(mesh):
     sizes = (mesh.shape["gx"], mesh.shape["gy"], mesh.shape["gz"])
     nx, ny, nz = sizes
-    share = SUMS // nz // nx
+    share = FIRST_SUMS // nx
     cells = PLANES * 16 * LANES * nx * ny * nz
     scale = 1.0 / (time_step * math.sqrt(float(cells)))
     vmem = pl.BlockSpec(memory_space=pltpu.VMEM)

time: 67.6 us -> 66.7 us (0.987)
  Pallas kernels: 66.8 us -> 66 us
    pallas_call x1, Pallas kernels: 65.4 us -> 64.5 us  [on_device(): pl.pallas_call(functools.partial(kernel, sizes, scale), out_shape=(buffer...]
where the time goes in v6:
time: 66.7 us; the launch traced here: 66.6 us
  Pallas kernels  66 us (99%)
    pallas_call x1, Pallas kernels, on_device(): pl.pallas_call(functools.partial(kernel, sizes, scale), out_shape=(buffer...  64.5 us
    pallas_call x1, Pallas kernels, on_device(): pl.pallas_call(deliver, out_shape=shapes, in_specs=[vmem] * 3, out_specs=...  1.41 us

profile of v6, /device:TPU:1, one launch (start us, length us, event | category | flops | bytes accessed | tf_op | source)
XLA Modules:
  0.0 66.6 jit_solution(13773086319709598451)
XLA Ops:
  0.6 64.5 %two_steps_and_adjoint.1 = (f32[4,6,16,128]{3,2,1,0:T(8,128)S(1)}, f32[4,6,16,128]{3,2,1,0:T(8,128)S(1)}, f32[320,128]{1,0:T(8,128)S(1)}) custom-call(f32[4,6,16,128]{3,2,1,0:T(8,128)} %state_in.1, f32[4,6,16,128]{3,2,1,0:T(8,128)} %cot_in.1, f32[6,16,128]{2,1,0:T(8,128)} %diff_in.1, bf16[40,128]{1,0:T(8,128)(2,1)} %w_in.1, bf16[128,128]{1,0:T(8,128)(2,1)} %w_second.1, ...), custom_call_target="tpu_custom_call" | custom-call | tf_op jit(solution)/shard_map/two_steps_and_adjoint/pallas_call | solution.py:982
  65.2 1.4 %deliver.1 = (f32[4,6,16,128]{3,2,1,0:T(8,128)}, f32[4,6,16,128]{3,2,1,0:T(8,128)}, f32[40,128]{1,0:T(8,128)}, f32[128,128]{1,0:T(8,128)}, f32[128,128]{1,0:T(8,...) custom-call(f32[4,6,16,128]{3,2,1,0:T(8,128)S(1)} %get-tuple-element.19.final_in, ...), custom_call_target="tpu_custom_call" | custom-call | tf_op jit(solution)/shard_map/deliver/pallas_call | solution.py:997
